TPU v7x, 256 devices: a whole 4x4x8 slice. The times are simulated.
256 devices in a mesh: segment: 8 (over z), ctx: 32 (over y, x, core).
Axes of the slice: x: 4, y: 4, z: 8, core: 2. Of those that a mesh axis runs over, the one named last changes fastest.
Arguments:
- acts: bfloat16 [8, 4096, 2048], P('segment', 'ctx'), may hold values from -10 to 10
- norm_gains: float32 [8, 3, 2048], P('segment'), may hold values from 0.25 to 1.75
- w_kv: bfloat16 [8, 2048, 1024], P('segment', None, 'ctx'), may hold values from -1 to 36.35534
- dt_in: bfloat16 [8, 2048, 128], P('segment'), may hold values from -0.125 to 0.125
- dt_out: bfloat16 [8, 128, 2048], P('segment'), may hold values from -0.5 to 0.5
- dt_bias: float32 [8, 2048], P('segment'), may hold values from -3 to -1
- decay_rate: float32 [8, 2048], P('segment'), may hold values from 0.002 to 2
- w_bc: bfloat16 [8, 2048, 32], P('segment'), may hold values from -0.03125 to 0.03125
- skip_gain: float32 [8, 2048], P('segment'), may hold values from 0.25 to 1.75
- w_router: bfloat16 [8, 2048, 4], P('segment'), may hold values from -1.109145 to 1.109145
- routes: int32 [8, 4096, 2], P('segment', 'ctx'), may hold values from 0 to 3, all different within a row; in each aligned block of 128 rows (0 to 127, 128 to 255, ..., all dimensions but the last counted through in order) at most 64 rows name the same one
- w_up: bfloat16 [8, 2048, 28672], P('segment', None, 'ctx'), may hold values from -0.125 to 0.125
- w_down: bfloat16 [8, 28672, 2048], P('segment', 'ctx'), may hold values from -0.0625 to 0.0625
Outputs:
- handed: bfloat16 [8, 4096, 2048], P('segment', 'ctx')
Inputs may be any that keep to these rules, and one draw needn't show every extreme that they name: `routes`: in each section, the 128 rows of one context shard name every expert exactly 64 times; a token's 2 experts differ.
All inputs are finite; a program needn't handle non-finite values.
Results may differ from a plain program's by a relative error of at most 0.017.
Values may be sent and summed in bfloat16 or wider, within the bound.
A program may use at most 128 MiB of HBM per device.

v0:
```python
import jax
import jax.numpy as jnp
from jax import lax
from jax.sharding import PartitionSpec as P

HEADS = 16
KVH = 4
HD = 128
EXPERTS = 4


def entering(array, axis, join, neutral):
    place = lax.axis_index(axis)
    gathered = jax.tree.map(
        lambda a, kind: lax.all_gather(a.astype(kind), axis), array, (jnp.bfloat16, jnp.bfloat16)
    )
    state = jax.tree.map(lambda a, e: jnp.zeros_like(a) + jnp.asarray(e, a.dtype), array, neutral)

    def one(turn, state):
        return join(
            state,
            jax.tree.map(
                lambda a, own: lax.dynamic_index_in_dim(a, turn, 0, False).astype(own.dtype),
                gathered,
                array,
            ),
        )

    return lax.fori_loop(0, place, one, state)


def shifted(value, axis, steps):
    count = lax.axis_size(axis)
    pairs = [(source, (source + steps) % count) for source in range(count)]
    return lax.ppermute(value, axis, pairs)


def rms_norm(values, gain):
    return values * lax.rsqrt(jnp.mean(values * values, -1, keepdims=True) + 1e-06) * gain


def combine_states(earlier, later):
    return (earlier[0] * later[0], later[0][:, None] * earlier[1] + later[1])


def on_device(
    acts,
    norm_gains,
    w_kv,
    dt_in,
    dt_out,
    dt_bias,
    decay_rate,
    w_bc,
    skip_gain,
    w_router,
    routes,
    w_up,
    w_down,
):
    shard_count = lax.axis_size("ctx")
    shard_index = lax.axis_index("ctx")
    start_x = acts[0].astype(jnp.float32)
    rows_here = start_x.shape[0]
    width = start_x.shape[1]
    group = HEADS // KVH
    normed = rms_norm(start_x, norm_gains[0, 0]).astype(jnp.bfloat16)
    kv_rows = jnp.dot(
        normed,
        lax.all_gather(w_kv[0], "ctx", axis=1, tiled=True),
        preferred_element_type=jnp.float32,
    ).astype(jnp.bfloat16)
    keys = kv_rows[:, : KVH * HD].reshape(rows_here, KVH, HD)
    values = kv_rows[:, KVH * HD :].reshape(rows_here, KVH, HD)
    queries = normed.reshape(rows_here, KVH, group, HD)
    query_pos = shard_index * rows_here + jnp.arange(rows_here, dtype=jnp.int32)
    running = jnp.full((rows_here, KVH, group), -1e30, jnp.float32)
    key_piece = lax.all_gather(keys, "ctx", axis=0, tiled=True)
    value_piece = lax.all_gather(values, "ctx", axis=0, tiled=True)
    key_pos = jnp.arange(key_piece.shape[0], dtype=jnp.int32)
    scores = jnp.einsum(
        "tgrd,sgd->tgrs", queries, key_piece, preferred_element_type=jnp.float32
    ) * HD ** (-0.5)
    allowed = (key_pos[None, :] <= query_pos[:, None])[:, None, None, :]
    scores = jnp.where(allowed, scores, -1e30)
    newest = jnp.maximum(running, jnp.max(scores, -1))
    weights = jnp.where(allowed, jnp.exp(scores - newest[..., None]), 0.0)
    total = jnp.sum(weights, -1)
    summed = jnp.einsum(
        "tgrs,sgd->tgrd",
        weights.astype(jnp.bfloat16),
        value_piece,
        preferred_element_type=jnp.float32,
    )
    _, total, summed = (newest, total, summed)
    first = start_x + (summed / total[..., None]).reshape(rows_here, width)
    mixed_in = rms_norm(first, norm_gains[0, 1]).astype(jnp.bfloat16)
    low_rank = jnp.dot(mixed_in, dt_in[0], preferred_element_type=jnp.float32).astype(jnp.bfloat16)
    step_size = jax.nn.softplus(
        jnp.dot(low_rank, dt_out[0], preferred_element_type=jnp.float32) + dt_bias[0]
    )
    log_decay = step_size * decay_rate[0]
    state_width = w_bc.shape[2] // 2
    both = jnp.dot(mixed_in, w_bc[0], preferred_element_type=jnp.float32)
    b_part = both[:, :state_width]
    c_part = both[:, state_width:]
    driven = step_size * mixed_in.astype(jnp.float32)
    block_rows = min(32, rows_here)
    block_count = rows_here // block_rows
    lower_mask = jnp.arange(block_rows)[:, None] >= jnp.arange(block_rows)[None, :]
    lower_float = lower_mask.astype(jnp.float32)

    def block_scan(carry, item):
        state, offset_sum = carry
        rate_block, drive_block, b_block, c_block = item
        running_sum = jnp.dot(lower_float, rate_block, precision=lax.Precision.HIGHEST)
        coupling = jnp.dot(c_block, b_block.T, precision=lax.Precision.HIGHEST)
        distance = jnp.maximum(running_sum[:, None, :] - running_sum[None, :, :], 0.0)
        fading = jnp.where(lower_mask[:, :, None], jnp.exp(-distance), 0.0)
        within = jnp.sum(fading * coupling[:, :, None] * drive_block[None, :, :], 1)
        decay_in = jnp.exp(-running_sum)
        from_state = jnp.dot(c_block, state.T, precision=lax.Precision.HIGHEST) * decay_in
        tail_weight = jnp.exp(running_sum - running_sum[-1][None, :]) * drive_block
        state = decay_in[-1][:, None] * state + jnp.dot(
            tail_weight.T, b_block, precision=lax.Precision.HIGHEST
        )
        shard_decay = jnp.exp(-(offset_sum[None, :] + running_sum))
        return ((state, offset_sum + running_sum[-1]), (within + from_state, shard_decay))

    start_carry = (jnp.zeros((width, state_width), jnp.float32), jnp.zeros((width,), jnp.float32))
    scan_items = (
        log_decay.reshape(block_count, block_rows, width),
        driven.reshape(block_count, block_rows, width),
        b_part.reshape(block_count, block_rows, state_width),
        c_part.reshape(block_count, block_rows, state_width),
    )
    (end_state, end_offset), (block_out, block_decay) = lax.scan(
        block_scan, start_carry, scan_items
    )
    local_out = block_out.reshape(rows_here, width)
    products = block_decay.reshape(rows_here, width)
    end_product = jnp.exp(-end_offset)
    identity = (jnp.ones((width,), jnp.float32), jnp.zeros((width, state_width), jnp.float32))
    incoming = entering((end_product, end_state), "ctx", combine_states, identity)[1]
    carried = jnp.dot(c_part, incoming.T, precision=lax.Precision.HIGHEST) * products
    second = first + local_out + carried + skip_gain[0] * mixed_in.astype(jnp.float32)
    expert_in = rms_norm(second, norm_gains[0, 2]).astype(jnp.bfloat16)
    logits = jnp.dot(expert_in, w_router[0], preferred_element_type=jnp.float32)
    top_count = routes.shape[2]
    expert_ids = jnp.arange(EXPERTS, dtype=jnp.int32)
    picked = (routes[0][:, :, None] == expert_ids[None, None, :]).astype(jnp.float32)
    chosen = jnp.sum(picked * logits[:, None, :], -1)
    gates = jax.nn.softmax(chosen, -1)
    flat_route = routes[0].reshape(-1)
    flat_hits = (flat_route[:, None] == expert_ids[None, :]).astype(jnp.int32)
    earlier_hits = jnp.cumsum(flat_hits, 0) - flat_hits
    slot_rank = jnp.sum(earlier_hits * flat_hits, -1)
    capacity = rows_here * top_count // EXPERTS
    parts = shard_count // EXPERTS
    position = flat_route * capacity + slot_rank
    slot_ids = jnp.arange(EXPERTS * capacity, dtype=jnp.int32)
    placing = (position[None, :] == slot_ids[:, None]).astype(jnp.bfloat16)
    repeated = jnp.repeat(expert_in, top_count, 0)
    packed = (
        jnp.dot(placing, repeated, preferred_element_type=jnp.float32)
        .astype(jnp.bfloat16)
        .reshape(EXPERTS, capacity, width)
    )
    up_local = w_up[0]
    down_local = w_down[0]
    outgoing = jnp.repeat(packed, parts, 0)
    received = lax.all_to_all(outgoing, "ctx", split_axis=0, concat_axis=0, tiled=True)
    flat_rows = received.reshape(-1, width)
    hidden = jax.nn.silu(jnp.dot(flat_rows, up_local, preferred_element_type=jnp.float32)).astype(
        jnp.bfloat16
    )
    part_out = (
        jnp.dot(hidden, down_local, preferred_element_type=jnp.float32)
        .astype(jnp.bfloat16)
        .reshape(received.shape)
    )
    returned = lax.all_to_all(part_out, "ctx", split_axis=0, concat_axis=0, tiled=True)
    expert_out = (
        returned.reshape(EXPERTS, parts, capacity, width)
        .astype(jnp.float32)
        .sum(1)
        .reshape(EXPERTS * capacity, width)
    )
    weighting = (position[:, None] == slot_ids[None, :]).astype(jnp.float32) * gates.reshape(-1)[
        :, None
    ]
    moe_rows = (
        jnp.dot(weighting, expert_out, precision=lax.Precision.HIGHEST)
        .reshape(rows_here, top_count, width)
        .sum(1)
    )
    finished = (second + moe_rows).astype(jnp.bfloat16)
    return shifted(finished[None], "segment", 1)


def solution(mesh):
    in_specs = (
        P("segment", "ctx", None),
        P("segment", None, None),
        P("segment", None, "ctx"),
        P("segment", None, None),
        P("segment", None, None),
        P("segment", None),
        P("segment", None),
        P("segment", None, None),
        P("segment", None),
        P("segment", None, None),
        P("segment", "ctx", None),
        P("segment", None, "ctx"),
        P("segment", "ctx", None),
    )
    out_specs = P("segment", "ctx", None)
    return jax.shard_map(
        on_device, mesh=mesh, in_specs=in_specs, out_specs=out_specs, check_vma=False
    )
```

profile of v0, /device:TPU:1, one launch (start us, length us, event | category | flops | bytes accessed | tf_op | source)
XLA Modules:
  0.0 546.6 jit_solution(13413546750977769218)
XLA Ops:
  9.3 56.0 %all-gather.12.cloned.1.call-done = bf16[1,2048,1024]{1,2,0:T(8,128)(2,1)} async-done(((bf16[1,2048,32]{1,2,0:T(8,128)(2,1)}), bf16[1,2048,1024]{1,2,0:T(8,128)(2,1)}) %all-gather.12.cloned.1.call-update) | async-done | bytes 4194320 | tf_op jit(solution)/shard_map/all_gather | solution.py:70
  65.3 3.9 fusion.50
  72.4 48.1 %all-gather.10.cloned.1.call-done = bf16[4096,4,128]{2,0,1:T(8,128)(2,1)} async-done(((bf16[128,4,128]{2,0,1:T(8,128)(2,1)}), bf16[4096,4,128]{2,0,1:T(8,128)(2,1)}) %all-gather.10.cloned.1.call-update) | async-done | bytes 4194320 | tf_op jit(solution)/shard_map/all_gather | solution.py:78
  120.6 15.7 %fusion.19 = (f32[128,4,4]{0,2,1:T(4,128)S(1)}, f32[4,4096,128,4]{2,1,3,0:T(8,128)}) fusion(pred[128,4096]{0,1:T(8,128)(4,1)S(1)} %iota_compare_fusion.2, f32[128,4,4,128]{0,3,2,1:T(8,128)S(1)} %bitcast.225, f32[4,4,128]{2,1,0:T(4,128)S(1)} %bitcast.246, f32[128]{0:T(128)S(1)} %add_rsqrt_fusion.2, bf16[4096,4,128]{2,0,1:T(8,128)(2,1)} %all-gather.10.cloned.1.call-done), kind=kOutput, calls=%fused_computation.32 | convolution fusion | flops 2173433856 | bytes 39338496 | tf_op jit(solution)/shard_map/tgrd,sgd->tgrs/dot_general | solution.py:81
  136.2 14.7 %fusion.20 = f32[128,4,4]{0,2,1:T(4,128)S(1)} fusion(f32[4,4096,128,4]{2,1,3,0:T(8,128)} %get-tuple-element.251, f32[128,4,4]{0,2,1:T(4,128)S(1)} %broadcast_maximum_fusion, pred[128,4096]{0,1:T(8,128)(4,1)S(1)} %iota_compare_fusion.2), kind=kLoop, calls=%fused_computation.33 | loop fusion | flops 41940992 | bytes 34095104 | tf_op jit(solution)/shard_map/reduce_sum | solution.py:88
  151.0 25.8 %all-gather.8.cloned.1.call-done = bf16[4096,4,128]{0,2,1:T(8,128)(2,1)} async-done(((bf16[128,4,128]{0,2,1:T(8,128)(2,1)}), bf16[4096,4,128]{0,2,1:T(8,128)(2,1)}) %all-gather.8.cloned.1.call-update) | async-done | bytes 4194320 | tf_op jit(solution)/shard_map/all_gather | solution.py:79
  176.8 16.8 %multiply_reduce_fusion.2 = (f32[128]{0:T(128)S(1)}, f32[128,4,4,128]{0,3,2,1:T(8,128)}, f32[128,4,4,128]{0,3,2,1:T(8,128)}) fusion(f32[128,4,4,128]{0,3,2,1:T(8,128)S(1)} %bitcast.226, f32[128,4,4]{0,2,1:T(4,128)S(1)} %fusion.20, f32[4,4096,128,4]{2,1,3,0:T(8,128)} %get-tuple-element.251, f32[128,4,4]{0,2,1:T(4,128)S(1)} %broadcast_maximum_fusion, ...), kind=kOutput, calls=%fused_computation.76 | convolution fusion | flops 2190475264 | bytes 41435648 | tf_op jit(solution)/shard_map/tgrs,sgd->tgrd/dot_general | solution.py:89
  197.1 3.8 convert_multiply_fusion.1
  201.0 30.0 %while.30 = (s32[]{:T(128)}, f32[2048,16]{0,1:T(8,128)S(1)}, f32[2048]{0:T(1024)S(1)}, f32[4,32,2048]{2,1,0:T(8,128)}, f32[4,32,2048]{2,1,0:T(8,128)}, /*index=5...) while((s32[]{:T(128)}, f32[2048,16]{0,1:T(8,128)S(1)}, ...), condition=%wide.region_6.7_spmd.clone, body=%wide.region_4.6_spmd.clone.sunk | while | flops 65805312 | bytes 4443777 | solution.py:137
  203.5 2.7 multiply_reduce_fusion.4
  211.0 2.7 multiply_reduce_fusion.4
  218.5 2.7 multiply_reduce_fusion.4
  226.0 2.7 multiply_reduce_fusion.4
  233.7 24.0 %all-gather.1 = bf16[65536]{0:T(1024)(128)(2,1)S(1)} all-gather(bf16[2048]{0:T(1024)(128)(2,1)S(1)} %exponential_convert_fusion), channel_id=3, replica_groups=mesh['segment'=8,'ctx'=32] {'ctx'}, dimensions={0}, use_global_device_ids=true | all-gather | bytes 135168 | tf_op jit(solution)/shard_map/all_gather | solution.py:15
  259.2 21.1 %all-gather.14.cloned.1.call-done = bf16[65536,16]{0,1:T(8,128)(2,1)} async-done(((bf16[2048,16]{0,1:T(8,128)(2,1)}), bf16[65536,16]{0,1:T(8,128)(2,1)}) %all-gather.14.cloned.1.call-update) | async-done | bytes 2097168 | tf_op jit(solution)/shard_map/all_gather | solution.py:15
  280.2 1.8 copy.88
  282.2 2.7 multiply_reduce_fusion.1
  289.7 103.0 %all_to_all.10 = bf16[32,64,2048]{2,1,0:T(8,128)(2,1)} all-to-all(bf16[32,64,2048]{2,1,0:T(8,128)(2,1)S(1)} %bitcast.219), channel_id=1, replica_groups=mesh['segment'=8,'ctx'=32] {'ctx'}, dimensions={0} | all-to-all | bytes 16777216 | tf_op jit(solution)/shard_map/all_to_all | solution.py:172
  392.7 24.2 %convolution_convert_fusion = bf16[2048,2048]{1,0:T(8,128)(2,1)} fusion(bf16[1,896,2048]{2,1,0:T(8,128)(2,1)} %param.29, bf16[2048,2048]{1,0:T(8,128)(2,1)} %bitcast.222, bf16[1,2048,896]{2,1,0:T(8,128)(2,1)} %param.28), kind=kOutput, calls=%fused_computation.38 | convolution fusion | flops 15045754880 | bytes 24117248 | tf_op jit(solution)/shard_map/dot_general | solution.py:178
  416.9 5.3 all-to-all-start.1
  423.0 99.1 %all-to-all-done.1 = bf16[32,64,2048]{2,1,0:T(8,128)(2,1)} async-done(((bf16[32,64,2048]{2,1,0:T(8,128)(2,1)}), bf16[32,64,2048]{2,1,0:T(8,128)(2,1)}, u32[]{:S(2)}, u32[]{:S(2)}) %all-to-all-start.1) | async-done | bytes 8388640 | tf_op jit(solution)/shard_map/all_to_all | solution.py:182
  522.0 5.4 convert_reduce_fusion
  527.5 1.9 convolution_reduce_fusion
  530.9 8.3 %collective-permute-done = bf16[1,128,2048]{2,1,0:T(8,128)(2,1)S(1)} collective-permute-done((bf16[1,128,2048]{2,1,0:T(8,128)(2,1)S(1)}, bf16[1,128,2048]{2,1,0:T(8,128)(2,1)S(1)}, u32[]{:S(2)}, u32[]{:S(2)}) %collective-permute-start) | collective-permute-done | bytes 524320 | tf_op jit(solution)/shard_map/ppermute | solution.py:35
  (130 shorter events, 40.4 us)
Async XLA Ops:
  6.5 190.6 %copy-start = (bf16[1,128,2048]{2,1,0:T(8,128)(2,1)S(1)}, bf16[1,128,2048]{2,1,0:T(8,128)(2,1)}, u32[]{:S(2)}) copy-start(bf16[1,128,2048]{2,1,0:T(8,128)(2,1)} %param.21) | copy-start | bytes 1572868
  6.5 58.7 %all-gather.12.cloned.1.call-start = ((), (), s32[]{:S(2)}) async-start(), calls=%async_computation.4 | async-start | bytes 4325376 | tf_op jit(solution)/shard_map/all_gather | solution.py:70
  7.3 113.3 %all-gather.10.cloned.1.call-start = ((), (), s32[]{:S(2)}) async-start(), calls=%async_computation.3 | async-start | bytes 4325376 | tf_op jit(solution)/shard_map/all_gather | solution.py:78
  69.9 106.9 %all-gather.8.cloned.1.call-start = ((), (), s32[]{:S(2)}) async-start(), calls=%async_computation.2 | async-start | bytes 4325376 | tf_op jit(solution)/shard_map/all_gather | solution.py:79
  70.7 209.5 %all-gather.14.cloned.1.call-start = ((), (), s32[]{:S(2)}) async-start(), calls=%async_computation.5 | async-start | bytes 2162688 | tf_op jit(solution)/shard_map/all_gather | solution.py:15
  150.9 45.8 %copy-start.3 = (bf16[1,2048,32]{1,2,0:T(8,128)(2,1)S(1)}, bf16[1,2048,32]{1,2,0:T(8,128)(2,1)}, u32[]{:S(2)}) copy-start(bf16[1,2048,32]{1,2,0:T(8,128)(2,1)} %param.24) | copy-start | bytes 393220
  151.0 46.2 %copy-start.2 = (bf16[1,128,2048]{2,1,0:T(8,128)(2,1)S(1)}, bf16[1,128,2048]{2,1,0:T(8,128)(2,1)}, u32[]{:S(2)}) copy-start(bf16[1,128,2048]{2,1,0:T(8,128)(2,1)} %param.17) | copy-start | bytes 1572868
  151.0 46.1 %copy-start.5 = (f32[1,2048]{1,0:T(1,128)S(1)}, f32[1,2048]{1,0:T(1,128)}, u32[]{:S(2)}) copy-start(f32[1,2048]{1,0:T(1,128)} %param.23) | copy-start | bytes 24580
  151.0 46.1 %copy-start.6 = (f32[1,2048]{1,0:T(1,128)S(1)}, f32[1,2048]{1,0:T(1,128)}, u32[]{:S(2)}) copy-start(f32[1,2048]{1,0:T(1,128)} %param.22) | copy-start | bytes 24580
  201.0 30.6 %copy-start.8 = (s32[1,128,2]{1,2,0:T(2,128)S(1)}, s32[1,128,2]{1,2,0:T(2,128)}, u32[]{:S(2)}) copy-start(s32[1,128,2]{1,2,0:T(2,128)} %param.27) | copy-start | bytes 3076
  230.9 51.2 %copy-start.7 = (f32[1,2048]{1,0:T(1,128)S(1)}, f32[1,2048]{1,0:T(1,128)}, u32[]{:S(2)}) copy-start(f32[1,2048]{1,0:T(1,128)} %param.25) | copy-start | bytes 24580
  416.9 5.7 %copy-start.4 = (bf16[1,2048,4]{1,2,0:T(4,128)(2,1)S(1)}, bf16[1,2048,4]{1,2,0:T(4,128)(2,1)}, u32[]{:S(2)}) copy-start(bf16[1,2048,4]{1,2,0:T(4,128)(2,1)} %param.26) | copy-start | bytes 49156
  416.9 105.1 %all-to-all-start.1 = ((bf16[32,64,2048]{2,1,0:T(8,128)(2,1)}), bf16[32,64,2048]{2,1,0:T(8,128)(2,1)}, u32[]{:S(2)}, u32[]{:S(2)}) async-start(bf16[32,64,2048]{2,1,0:T(8,128)(2,1)} %bitcast.221), calls=%async_computation.1 | async-start | bytes 16777216 | tf_op jit(solution)/shard_map/all_to_all | solution.py:182
  422.9 117.1 %copy-start.1 = (bf16[1,128,2048]{2,1,0:T(8,128)(2,1)S(1)}, bf16[1,128,2048]{2,1,0:T(8,128)(2,1)}, u32[]{:S(2)}) copy-start(bf16[1,128,2048]{2,1,0:T(8,128)(2,1)} %param.21) | copy-start | bytes 1572868
  529.5 9.7 %collective-permute-start = (bf16[1,128,2048]{2,1,0:T(8,128)(2,1)S(1)}, bf16[1,128,2048]{2,1,0:T(8,128)(2,1)S(1)}, u32[]{:S(2)}, u32[]{:S(2)}) collective-permute-start(bf16[1,128,2048]{2,1,0:T(8,128)(2,1)S(1)} %fusion.56), channel_id=1, source_target_pairs={{0,32},{32,64},{64,96},{96,128},{128,160},{160,192},{192,224},{224... | collective-permute-start | bytes 1572872 | tf_op jit(solution)/shard_map/ppermute | solution.py:35
Sparse Core Ops, SparseCore 0:
  9.9 55.2 all-gather.11
  70.0 50.5 all-gather.9
  123.0 53.6 all-gather.7
  231.7 48.4 all-gather.13
where the time goes:
time: 553 us; the launch traced here: 547 us
  waiting for transfers between devices  259 us (47%)
  blocking collectives  127 us (23%)
  matrix products  83 us (15%)
  other arithmetic  40.9 us (7%)
  local copies, waits for them, and re-layouts  15.8 us (3%)
  between operations  13.5 us (2%)
  starting transfers between devices  6.83 us (1%)
    all_to_all x1, blocking collectives, on_device(): lax.all_to_all(outgoing, 'ctx', split_axis=0, concat_axis=0, tiled=True)  103 us
    all_to_all x1, waiting for transfers between devices, on_device(): lax.all_to_all(part_out, 'ctx', split_axis=0, concat_axis=0, tiled=True)  99.1 us
    all_gather x1, waiting for transfers between devices, on_device(): lax.all_gather(w_kv[0], 'ctx', axis=1, tiled=True)  56 us
    all_gather x1, waiting for transfers between devices, on_device(): key_piece = lax.all_gather(keys, 'ctx', axis=0, tiled=True)  48.1 us
    all_gather x1, waiting for transfers between devices, on_device(): value_piece = lax.all_gather(values, 'ctx', axis=0, tiled=True)  25.8 us
    dot_general x1, matrix products, on_device(): jnp.dot(hidden, down_local, preferred_element_type=jnp.float32)  24.2 us
    all_gather x1, blocking collectives, entering(): lax.all_gather(a.astype(kind), axis)  24 us
    all_gather x1, waiting for transfers between devices, entering(): lax.all_gather(a.astype(kind), axis)  21.1 us
  transfers between devices with their start and end apart: 6, of which 6 were waited for; matrix products, arithmetic and copies ran while one was open for 7% of the time, Pallas kernels for 0%

commit v1 on v0

--- a/solution.py
+++ b/solution.py
@@ -1,6 +1,10 @@
+import functools
+
 import jax
 import jax.numpy as jnp
 from jax import lax
+from jax.experimental import pallas as pl
+from jax.experimental.pallas import tpu as pltpu
 from jax.sharding import PartitionSpec as P
 
 HEADS = 16
@@ -41,6 +45,290 @@
 
 def combine_states(earlier, later):
     return (earlier[0] * later[0], later[0][:, None] * earlier[1] + later[1])
+
+
+X_CHIPS = 4
+Y_CHIPS = 4
+MIB = 1 << 20
+
+
+def place(y, x, core):
+    return {"ctx": (y * X_CHIPS + x) * 2 + core}
+
+
+def coordinates():
+    ctx = lax.axis_index("ctx")
+    return lax.div(ctx, 2 * X_CHIPS), lax.rem(lax.div(ctx, 2), X_CHIPS), lax.rem(ctx, 2)
+
+
+def greet(peers):
+    barrier = pltpu.get_barrier_semaphore()
+    for peer in peers:
+        pl.semaphore_signal(barrier, inc=1, device_id=peer, device_id_type=pl.DeviceIdType.MESH)
+    pl.semaphore_wait(barrier, len(peers))
+
+
+def moe_kernel(
+    packed,
+    up_any,
+    down_any,
+    out,
+    rows,
+    parts,
+    sibling_parts,
+    far_parts,
+    side_parts,
+    up,
+    down,
+    hidden,
+    weight_sem,
+    send_y,
+    recv_y,
+    send_side,
+    recv_side,
+    send_far,
+    recv_far,
+    send_core,
+    recv_core,
+    back_core_send,
+    back_core_recv,
+    back_far_send,
+    back_far_recv,
+    back_side_send,
+    back_side_recv,
+    back_y_send,
+    back_y_recv,
+):
+    y, x, core = coordinates()
+    left = lax.rem(x + X_CHIPS - 1, X_CHIPS)
+    right = lax.rem(x + 1, X_CHIPS)
+    far = lax.rem(x + 2, X_CHIPS)
+    chips = (x, left, right, far)
+    on_left, on_right, on_core = place(y, left, core), place(y, right, core), place(y, x, 1 - core)
+    started = []
+
+    def row_of(k):
+        return lax.rem(y + k, Y_CHIPS)
+
+    def send(src, dst, send_sem, recv_sem, to):
+        copy = pltpu.make_async_remote_copy(
+            src_ref=src,
+            dst_ref=dst,
+            send_sem=send_sem,
+            recv_sem=recv_sem,
+            device_id=to,
+            device_id_type=pl.DeviceIdType.MESH,
+        )
+        copy.start()
+        started.append(copy)
+
+    def arrived(dst, sem):
+        pltpu.make_async_copy(dst, dst, sem).wait()
+
+    load_up = pltpu.make_async_copy(up_any, up, weight_sem.at[0])
+    load_down = pltpu.make_async_copy(down_any, down, weight_sem.at[1])
+    load_up.start()
+    load_down.start()
+    greet([on_left, on_right, on_core] + [place(row_of(k), x, core) for k in (1, 2, 3)])
+
+    def block(at, k):
+        return rows.at[chips[at], core, row_of(k)]
+
+    def own_block(k):
+        send(block(0, k), block(0, k), send_side.at[0, k], recv_side.at[0, k], on_right)
+        send(block(0, k), block(0, k), send_side.at[1, k], recv_side.at[1, k], on_left)
+        send(block(0, k), block(0, k), send_core.at[0, k], recv_core.at[0, k], on_core)
+
+    def side_block(k):
+        arrived(block(1, k), recv_side.at[0, k])
+        if k in (0, 1):
+            send(block(1, k), block(1, k), send_far.at[k], recv_far.at[k], on_right)
+        send(block(1, k), block(1, k), send_core.at[1, k], recv_core.at[1, k], on_core)
+        arrived(block(2, k), recv_side.at[1, k])
+        if k in (2, 3):
+            send(block(2, k), block(2, k), send_far.at[k], recv_far.at[k], on_left)
+        send(block(2, k), block(2, k), send_core.at[2, k], recv_core.at[2, k], on_core)
+
+    def far_block(k):
+        arrived(block(3, k), recv_far.at[k])
+        send(block(3, k), block(3, k), send_core.at[3, k], recv_core.at[3, k], on_core)
+
+    def from_core(at):
+        for k in range(Y_CHIPS):
+            other = rows.at[chips[at], 1 - core, row_of(k)]
+            arrived(other, recv_core.at[at, k])
+
+    def experts(at):
+        chip = chips[at]
+
+        def one_core(turn, carry):
+            which = lax.rem(1 - core + turn, 2)
+            taken = rows[chip, which].reshape(-1, rows.shape[-1])
+            lifted = jnp.dot(taken, up[...], preferred_element_type=jnp.float32)
+            hidden[...] = jax.nn.silu(lifted).astype(jnp.bfloat16)
+
+            def columns(j, carry):
+                span = pl.ds(pl.multiple_of(j * 512, 512), 512)
+                lowered = jnp.dot(hidden[...], down[:, span], preferred_element_type=jnp.float32)
+                parts[chip, which, :, :, span] = lowered.astype(jnp.bfloat16).reshape(
+                    Y_CHIPS, -1, 512
+                )
+                return carry
+
+            return lax.fori_loop(0, rows.shape[-1] // 512, columns, carry)
+
+        lax.fori_loop(0, 2, one_core, 0)
+        send(
+            parts.at[chip, 1 - core],
+            sibling_parts.at[chip],
+            back_core_send.at[at],
+            back_core_recv.at[at],
+            on_core,
+        )
+
+    def added(*refs):
+        total = refs[0][...].astype(jnp.float32)
+        for ref in refs[1:]:
+            total = total + ref[...].astype(jnp.float32)
+        return total.astype(jnp.bfloat16)
+
+    def mine(at, k):
+        return parts.at[chips[at], core, row_of(k)]
+
+    def theirs(at, k):
+        return sibling_parts.at[chips[at], row_of(k)]
+
+    for k in (1, 3, 2):
+        send(
+            packed.at[row_of(k)],
+            rows.at[x, core, y],
+            send_y.at[k],
+            recv_y.at[4 - k],
+            place(row_of(k), x, core),
+        )
+    rows[x, core, y] = packed[y]
+    own_block(0)
+    for k in (1, 3, 2):
+        arrived(block(0, k), recv_y.at[k])
+        own_block(k)
+    load_up.wait()
+    load_down.wait()
+    from_core(0)
+    side_block(0)
+    experts(0)
+    for k in (1, 3, 2):
+        side_block(k)
+    from_core(1)
+    experts(1)
+    far_block(0)
+    from_core(2)
+    experts(2)
+    for k in (1, 3, 2):
+        far_block(k)
+
+    def core_sum(at):
+        arrived(sibling_parts.at[chips[at]], back_core_recv.at[at])
+
+    def to_side(at, k, relayed):
+        if relayed:
+            slot = far_parts.at[k]
+            arrived(slot, back_far_recv.at[k])
+            mine(at, k)[...] = added(mine(at, k), theirs(at, k), slot)
+        else:
+            mine(at, k)[...] = added(mine(at, k), theirs(at, k))
+        to = on_left if at == 1 else on_right
+        send(
+            mine(at, k),
+            side_parts.at[at - 1, k],
+            back_side_send.at[at - 1, k],
+            back_side_recv.at[at - 1, k],
+            to,
+        )
+
+    core_sum(1)
+    core_sum(2)
+    for k in (3, 0):
+        to_side(1, k, False)
+    for k in (2, 1):
+        to_side(2, k, False)
+    from_core(3)
+    experts(3)
+    core_sum(3)
+    for k in (2, 3, 1, 0):
+        mine(3, k)[...] = added(mine(3, k), theirs(3, k))
+        to = on_left if k in (2, 1) else on_right
+        send(mine(3, k), far_parts.at[k], back_far_send.at[k], back_far_recv.at[k], to)
+    core_sum(0)
+    for k in (2, 3, 1, 0):
+        to_side(1 if k in (2, 1) else 2, k, True)
+    for k in (2, 3, 1, 0):
+        for at in (1, 2):
+            arrived(side_parts.at[at - 1, k], back_side_recv.at[at - 1, k])
+        total = added(mine(0, k), theirs(0, k), side_parts.at[0, k], side_parts.at[1, k])
+        if k == 0:
+            out[y] = total
+        else:
+            mine(0, k)[...] = total
+            send(
+                mine(0, k),
+                out.at[y],
+                back_y_send.at[k],
+                back_y_recv.at[4 - k],
+                place(row_of(k), x, core),
+            )
+    for k in (1, 3, 2):
+        arrived(out.at[row_of(k)], back_y_recv.at[k])
+    for copy in started:
+        copy.wait_send()
+
+
+def mixture(packed, w_up, w_down):
+    experts, capacity, width = packed.shape
+    units = w_up.shape[1]
+    kind = jnp.bfloat16
+    block = (capacity, width)
+    dma = pltpu.SemaphoreType.DMA
+    return pl.pallas_call(
+        moe_kernel,
+        out_shape=jax.ShapeDtypeStruct(packed.shape, kind),
+        in_specs=[
+            pl.BlockSpec(memory_space=pltpu.VMEM),
+            pl.BlockSpec(memory_space=pl.ANY),
+            pl.BlockSpec(memory_space=pl.ANY),
+        ],
+        out_specs=pl.BlockSpec(memory_space=pltpu.VMEM),
+        scratch_shapes=[
+            pltpu.VMEM((X_CHIPS, 2, Y_CHIPS) + block, kind),
+            pltpu.VMEM((X_CHIPS, 2, Y_CHIPS) + block, kind),
+            pltpu.VMEM((X_CHIPS, Y_CHIPS) + block, kind),
+            pltpu.VMEM((Y_CHIPS,) + block, kind),
+            pltpu.VMEM((2, Y_CHIPS) + block, kind),
+            pltpu.VMEM(w_up.shape, kind),
+            pltpu.VMEM(w_down.shape, kind),
+            pltpu.VMEM((Y_CHIPS * capacity, units), kind),
+            dma((2,)),
+            dma((4,)),
+            dma((4,)),
+            dma((2, 4)),
+            dma((2, 4)),
+            dma((4,)),
+            dma((4,)),
+            dma((4, 4)),
+            dma((4, 4)),
+            dma((4,)),
+            dma((4,)),
+            dma((4,)),
+            dma((4,)),
+            dma((2, 4)),
+            dma((2, 4)),
+            dma((4,)),
+            dma((4,)),
+        ],
+        compiler_params=pltpu.CompilerParams(
+            collective_id=1, has_side_effects=True, vmem_limit_bytes=56 * MIB
+        ),
+        name="mixture",
+    )(packed, w_up, w_down)
 
 
 def on_device(
@@ -58,7 +346,6 @@
     w_up,
     w_down,
 ):
-    shard_count = lax.axis_size("ctx")
     shard_index = lax.axis_index("ctx")
     start_x = acts[0].astype(jnp.float32)
     rows_here = start_x.shape[0]
@@ -156,7 +443,6 @@
     earlier_hits = jnp.cumsum(flat_hits, 0) - flat_hits
     slot_rank = jnp.sum(earlier_hits * flat_hits, -1)
     capacity = rows_here * top_count // EXPERTS
-    parts = shard_count // EXPERTS
     position = flat_route * capacity + slot_rank
     slot_ids = jnp.arange(EXPERTS * capacity, dtype=jnp.int32)
     placing = (position[None, :] == slot_ids[:, None]).astype(jnp.bfloat16)
@@ -166,24 +452,9 @@
         .astype(jnp.bfloat16)
         .reshape(EXPERTS, capacity, width)
     )
-    up_local = w_up[0]
-    down_local = w_down[0]
-    outgoing = jnp.repeat(packed, parts, 0)
-    received = lax.all_to_all(outgoing, "ctx", split_axis=0, concat_axis=0, tiled=True)
-    flat_rows = received.reshape(-1, width)
-    hidden = jax.nn.silu(jnp.dot(flat_rows, up_local, preferred_element_type=jnp.float32)).astype(
-        jnp.bfloat16
-    )
-    part_out = (
-        jnp.dot(hidden, down_local, preferred_element_type=jnp.float32)
-        .astype(jnp.bfloat16)
-        .reshape(received.shape)
-    )
-    returned = lax.all_to_all(part_out, "ctx", split_axis=0, concat_axis=0, tiled=True)
     expert_out = (
-        returned.reshape(EXPERTS, parts, capacity, width)
+        mixture(packed, w_up[0], w_down[0])
         .astype(jnp.float32)
-        .sum(1)
         .reshape(EXPERTS * capacity, width)
     )
     weighting = (position[:, None] == slot_ids[None, :]).astype(jnp.float32) * gates.reshape(-1)[

time: 553 us -> 438 us (0.79)
  Pallas kernels: 0 us -> 119 us
  blocking collectives: 127 us -> 24 us
  waiting for transfers between devices: 259 us -> 165 us
  matrix products: 83 us -> 60.1 us
    pallas_call x0 -> x1, Pallas kernels: none -> 119 us  [mixture(): pl.pallas_call(moe_kernel, out_shape=jax.ShapeDtypeStruct(packed.shape, k...]
    all_to_all x1 -> x0, blocking collectives: 103 us -> none  [on_device(): lax.all_to_all(outgoing, 'ctx', split_axis=0, concat_axis=0, tiled=True)]
    all_to_all x1 -> x0, waiting for transfers between devices: 99.1 us -> none  [on_device(): lax.all_to_all(part_out, 'ctx', split_axis=0, concat_axis=0, tiled=True)]
    dot_general x1 -> x0, matrix products: 24.2 us -> none  [on_device(): jnp.dot(hidden, down_local, preferred_element_type=jnp.float32)]
  transfers between devices with their start and end apart: 6 -> 5, of which waited for: 6 -> 5; matrix products, arithmetic and copies ran while one was open for 7% -> 9% of each run, Pallas kernels for 0% -> 0%
where the time goes in v1:
time: 438 us; the launch traced here: 436 us
  waiting for transfers between devices  165 us (38%)
  Pallas kernels  119 us (27%)
  matrix products  60.1 us (14%)
  other arithmetic  36.3 us (8%)
  blocking collectives  24 us (5%)
  local copies, waits for them, and re-layouts  16.3 us (4%)
  between operations  13.5 us (3%)
    pallas_call x1, Pallas kernels, mixture(): pl.pallas_call(moe_kernel, out_shape=jax.ShapeDtypeStruct(packed.shape, k...  119 us
    all_gather x1, waiting for transfers between devices, on_device(): lax.all_gather(w_kv[0], 'ctx', axis=1, tiled=True)  56 us
    all_gather x1, waiting for transfers between devices, on_device(): key_piece = lax.all_gather(keys, 'ctx', axis=0, tiled=True)  48.1 us
    all_gather x1, waiting for transfers between devices, on_device(): value_piece = lax.all_gather(values, 'ctx', axis=0, tiled=True)  25.8 us
    all_gather x1, blocking collectives, entering(): lax.all_gather(a.astype(kind), axis)  24 us
    all_gather x1, waiting for transfers between devices, entering(): lax.all_gather(a.astype(kind), axis)  20.8 us
    dot_general x1, matrix products, on_device(): jnp.einsum('tgrs,sgd->tgrd', weights.astype(jnp.bfloat16), value_piece, p...  16.8 us
    dot_general x1, matrix products, on_device(): jnp.einsum('tgrd,sgd->tgrs', queries, key_piece, preferred_element_type=j...  15.7 us
  transfers between devices with their start and end apart: 5, of which 5 were waited for; matrix products, arithmetic and copies ran while one was open for 9% of the time, Pallas kernels for 0%

profile of v1, /device:TPU:1, one launch (start us, length us, event | category | flops | bytes accessed | tf_op | source)
XLA Modules:
  0.0 436.0 jit_solution(5224348045491038180)
XLA Ops:
  9.3 56.0 %all-gather.12.cloned.1.call-done = bf16[1,2048,1024]{1,2,0:T(8,128)(2,1)} async-done(((bf16[1,2048,32]{1,2,0:T(8,128)(2,1)}), bf16[1,2048,1024]{1,2,0:T(8,128)(2,1)}) %all-gather.12.cloned.1.call-update) | async-done | bytes 4194320 | tf_op jit(solution)/shard_map/all_gather | solution.py:357
  65.3 3.9 fusion.42
  72.4 48.1 %all-gather.10.cloned.1.call-done = bf16[4096,4,128]{2,0,1:T(8,128)(2,1)} async-done(((bf16[128,4,128]{2,0,1:T(8,128)(2,1)}), bf16[4096,4,128]{2,0,1:T(8,128)(2,1)}) %all-gather.10.cloned.1.call-update) | async-done | bytes 4194320 | tf_op jit(solution)/shard_map/all_gather | solution.py:365
  120.6 15.7 %fusion.19 = (f32[128,4,4]{0,2,1:T(4,128)S(1)}, f32[4,4096,128,4]{2,1,3,0:T(8,128)}) fusion(pred[128,4096]{0,1:T(8,128)(4,1)S(1)} %iota_compare_fusion.2, f32[128,4,4,128]{0,3,2,1:T(8,128)S(1)} %bitcast.209, f32[4,4,128]{2,1,0:T(4,128)S(1)} %bitcast.232, f32[128]{0:T(128)S(1)} %add_rsqrt_fusion.2, bf16[4096,4,128]{2,0,1:T(8,128)(2,1)} %all-gather.10.cloned.1.call-done), kind=kOutput, calls=%fused_computation.32 | convolution fusion | flops 2173433856 | bytes 39338496 | tf_op jit(solution)/shard_map/tgrd,sgd->tgrs/dot_general | solution.py:368
  136.2 14.7 %fusion.20 = f32[128,4,4]{0,2,1:T(4,128)S(1)} fusion(f32[4,4096,128,4]{2,1,3,0:T(8,128)} %get-tuple-element.251, f32[128,4,4]{0,2,1:T(4,128)S(1)} %broadcast_maximum_fusion, pred[128,4096]{0,1:T(8,128)(4,1)S(1)} %iota_compare_fusion.2), kind=kLoop, calls=%fused_computation.33 | loop fusion | flops 41940992 | bytes 34095104 | tf_op jit(solution)/shard_map/reduce_sum | solution.py:375
  151.0 25.8 %all-gather.8.cloned.1.call-done = bf16[4096,4,128]{0,2,1:T(8,128)(2,1)} async-done(((bf16[128,4,128]{0,2,1:T(8,128)(2,1)}), bf16[4096,4,128]{0,2,1:T(8,128)(2,1)}) %all-gather.8.cloned.1.call-update) | async-done | bytes 4194320 | tf_op jit(solution)/shard_map/all_gather | solution.py:366
  176.8 16.8 %multiply_reduce_fusion.2 = (f32[128]{0:T(128)S(1)}, f32[128,4,4,128]{0,3,2,1:T(8,128)}, f32[128,4,4,128]{0,3,2,1:T(8,128)}) fusion(f32[128,4,4,128]{0,3,2,1:T(8,128)S(1)} %bitcast.210, f32[128,4,4]{0,2,1:T(4,128)S(1)} %fusion.20, f32[4,4096,128,4]{2,1,3,0:T(8,128)} %get-tuple-element.251, f32[128,4,4]{0,2,1:T(4,128)S(1)} %broadcast_maximum_fusion, ...), kind=kOutput, calls=%fused_computation.69 | convolution fusion | flops 2190475264 | bytes 41435648 | tf_op jit(solution)/shard_map/tgrs,sgd->tgrd/dot_general | solution.py:376
  193.6 1.6 copy.64
  195.1 1.6 multiply_convert_fusion.2
  197.1 3.8 convert_multiply_fusion.1
  201.0 29.9 %while.30 = (s32[]{:T(128)}, f32[2048,16]{0,1:T(8,128)S(1)}, f32[2048]{0:T(1024)S(1)}, f32[4,32,2048]{2,1,0:T(8,128)}, f32[4,32,2048]{2,1,0:T(8,128)}, /*index=5...) while((s32[]{:T(128)}, f32[2048,16]{0,1:T(8,128)S(1)}, ...), condition=%wide.region_6.7_spmd.clone, body=%wide.region_4.6_spmd.clone.sunk | while | flops 65805312 | bytes 4443777 | solution.py:424
  203.5 2.7 multiply_reduce_fusion.4
  211.0 2.7 multiply_reduce_fusion.4
  218.5 2.7 multiply_reduce_fusion.4
  226.0 2.7 multiply_reduce_fusion.4
  233.9 24.0 %all-gather.1 = bf16[65536]{0:T(1024)(128)(2,1)S(1)} all-gather(bf16[2048]{0:T(1024)(128)(2,1)S(1)} %exponential_convert_fusion), channel_id=3, replica_groups=mesh['segment'=8,'ctx'=32] {'ctx'}, dimensions={0}, use_global_device_ids=true | all-gather | bytes 135168 | tf_op jit(solution)/shard_map/all_gather | solution.py:19
  259.4 20.8 %all-gather.14.cloned.1.call-done = bf16[65536,16]{0,1:T(8,128)(2,1)} async-done(((bf16[2048,16]{0,1:T(8,128)(2,1)}), bf16[65536,16]{0,1:T(8,128)(2,1)}) %all-gather.14.cloned.1.call-update) | async-done | bytes 2097168 | tf_op jit(solution)/shard_map/all_gather | solution.py:19
  280.3 3.2 copy.88
  284.4 2.7 multiply_reduce_fusion.1
  288.3 1.5 reshape.241
  289.7 2.7 convolution_convert_fusion
  292.4 118.7 %mixture.1 = bf16[4,64,2048]{2,1,0:T(8,128)(2,1)} custom-call(bf16[4,64,2048]{2,1,0:T(8,128)(2,1)} %bitcast.211, bf16[2048,896]{1,0:T(8,128)(2,1)} %bitcast.212, bf16[896,2048]{1,0:T(8,128)(2,1)} %bitcast.213), custom_call_target="tpu_custom_call" | custom-call | tf_op jit(solution)/shard_map/mixture/pallas_call | solution.py:291
  411.1 2.3 convolution_reduce_fusion
  415.0 13.7 %collective-permute-done = bf16[1,128,2048]{2,1,0:T(8,128)(2,1)S(1)} collective-permute-done((bf16[1,128,2048]{2,1,0:T(8,128)(2,1)S(1)}, bf16[1,128,2048]{2,1,0:T(8,128)(2,1)S(1)}, u32[]{:S(2)}, u32[]{:S(2)}) %collective-permute-start) | collective-permute-done | bytes 524320 | tf_op jit(solution)/shard_map/ppermute | solution.py:39
  (123 shorter events, 35.1 us)
Async XLA Ops:
  6.5 190.6 %copy-start = (bf16[1,128,2048]{2,1,0:T(8,128)(2,1)S(1)}, bf16[1,128,2048]{2,1,0:T(8,128)(2,1)}, u32[]{:S(2)}) copy-start(bf16[1,128,2048]{2,1,0:T(8,128)(2,1)} %param.21) | copy-start | bytes 1572868
  6.5 58.7 %all-gather.12.cloned.1.call-start = ((), (), s32[]{:S(2)}) async-start(), calls=%async_computation.2 | async-start | bytes 4325376 | tf_op jit(solution)/shard_map/all_gather | solution.py:357
  7.3 113.3 %all-gather.10.cloned.1.call-start = ((), (), s32[]{:S(2)}) async-start(), calls=%async_computation.1 | async-start | bytes 4325376 | tf_op jit(solution)/shard_map/all_gather | solution.py:365
  69.9 106.9 %all-gather.8.cloned.1.call-start = ((), (), s32[]{:S(2)}) async-start(), calls=%async_computation | async-start | bytes 4325376 | tf_op jit(solution)/shard_map/all_gather | solution.py:366
  70.7 209.5 %all-gather.14.cloned.1.call-start = ((), (), s32[]{:S(2)}) async-start(), calls=%async_computation.3 | async-start | bytes 2162688 | tf_op jit(solution)/shard_map/all_gather | solution.py:19
  150.9 45.8 %copy-start.2 = (bf16[1,2048,32]{1,2,0:T(8,128)(2,1)S(1)}, bf16[1,2048,32]{1,2,0:T(8,128)(2,1)}, u32[]{:S(2)}) copy-start(bf16[1,2048,32]{1,2,0:T(8,128)(2,1)} %param.24) | copy-start | bytes 393220
  151.0 46.2 %copy-start.1 = (bf16[1,128,2048]{2,1,0:T(8,128)(2,1)S(1)}, bf16[1,128,2048]{2,1,0:T(8,128)(2,1)}, u32[]{:S(2)}) copy-start(bf16[1,128,2048]{2,1,0:T(8,128)(2,1)} %param.17) | copy-start | bytes 1572868
  151.0 46.1 %copy-start.4 = (f32[1,2048]{1,0:T(1,128)S(1)}, f32[1,2048]{1,0:T(1,128)}, u32[]{:S(2)}) copy-start(f32[1,2048]{1,0:T(1,128)} %param.23) | copy-start | bytes 24580
  151.0 46.1 %copy-start.5 = (f32[1,2048]{1,0:T(1,128)S(1)}, f32[1,2048]{1,0:T(1,128)}, u32[]{:S(2)}) copy-start(f32[1,2048]{1,0:T(1,128)} %param.22) | copy-start | bytes 24580
  201.0 30.6 %copy-start.7 = (s32[1,128,2]{1,2,0:T(2,128)S(1)}, s32[1,128,2]{1,2,0:T(2,128)}, u32[]{:S(2)}) copy-start(s32[1,128,2]{1,2,0:T(2,128)} %param.27) | copy-start | bytes 3076
  230.9 53.5 %copy-start.6 = (f32[1,2048]{1,0:T(1,128)S(1)}, f32[1,2048]{1,0:T(1,128)}, u32[]{:S(2)}) copy-start(f32[1,2048]{1,0:T(1,128)} %param.25) | copy-start | bytes 24580
  230.9 56.4 %copy-start.3 = (bf16[1,2048,4]{1,2,0:T(4,128)(2,1)S(1)}, bf16[1,2048,4]{1,2,0:T(4,128)(2,1)}, u32[]{:S(2)}) copy-start(bf16[1,2048,4]{1,2,0:T(4,128)(2,1)} %param.26) | copy-start | bytes 49156
  413.6 15.1 %collective-permute-start = (bf16[1,128,2048]{2,1,0:T(8,128)(2,1)S(1)}, bf16[1,128,2048]{2,1,0:T(8,128)(2,1)S(1)}, u32[]{:S(2)}, u32[]{:S(2)}) collective-permute-start(bf16[1,128,2048]{2,1,0:T(8,128)(2,1)S(1)} %fusion.48), channel_id=1, source_target_pairs={{0,32},{32,64},{64,96},{96,128},{128,160},{160,192},{192,224},{224... | collective-permute-start | bytes 1572872 | tf_op jit(solution)/shard_map/ppermute | solution.py:39
Sparse Core Ops, SparseCore 0:
  9.9 55.2 all-gather.11
  70.0 50.5 all-gather.9
  123.0 53.6 all-gather.7
  231.7 48.5 all-gather.13

commit v2 on v1

v2 whole, which is shorter than its diff:
```python
import jax
import jax.numpy as jnp
from jax import lax
from jax.experimental import pallas as pl
from jax.experimental.pallas import tpu as pltpu
from jax.sharding import PartitionSpec as P

HEADS = 16
KVH = 4
HD = 128
EXPERTS = 4
X_CHIPS = 4
Y_CHIPS = 4
MIB = 1 << 20
LOG2E = 1.4426950408889634


def place(y, x, core):
    return {"ctx": (y * X_CHIPS + x) * 2 + core}


def coordinates():
    ctx = lax.axis_index("ctx")
    return lax.div(ctx, 2 * X_CHIPS), lax.rem(lax.div(ctx, 2), X_CHIPS), lax.rem(ctx, 2)


def greet(peers):
    barrier = pltpu.get_barrier_semaphore()
    for peer in peers:
        pl.semaphore_signal(barrier, inc=1, device_id=peer, device_id_type=pl.DeviceIdType.MESH)


def greeted(count):
    pl.semaphore_wait(pltpu.get_barrier_semaphore(), count)


def arrived(dst, sem):
    pltpu.make_async_copy(dst, dst, sem).wait()


def rms_norm(values, gain):
    return values * lax.rsqrt(jnp.mean(values * values, -1, keepdims=True) + 1e-06) * gain


class Sender:
    def __init__(self):
        self.started = []

    def __call__(self, src, dst, send_sem, recv_sem, to):
        copy = pltpu.make_async_remote_copy(
            src_ref=src,
            dst_ref=dst,
            send_sem=send_sem,
            recv_sem=recv_sem,
            device_id=to,
            device_id_type=pl.DeviceIdType.MESH,
        )
        copy.start()
        self.started.append(copy)

    def finish(self):
        for copy in self.started:
            copy.wait_send()


class Gather:
    def __init__(self, buf, sems, send):
        self.buf, self.send = buf, send
        self.s1, self.r1, self.s2, self.r2, self.sc, self.rc = sems
        self.y, self.x, self.core = coordinates()

    def near(self, half, step, first):
        along_x = (half == 0) == first
        if along_x:
            return place(self.y, lax.rem(self.x + step, X_CHIPS), self.core)
        return place(lax.rem(self.y + step, Y_CHIPS), self.x, self.core)

    def block(self, half, step):
        if half == 0:
            return self.buf.at[self.y, lax.rem(self.x + step, X_CHIPS), self.core, 0]
        return self.buf.at[lax.rem(self.y + step, Y_CHIPS), self.x, self.core, 1]

    def line(self, half, step, pair=None, other=False):
        span = slice(None) if pair is None else pl.ds(2 * pair, 2)
        core = 1 - self.core if other else self.core
        if half == 0:
            return self.buf.at[lax.rem(self.y + step, Y_CHIPS), span, core, 0]
        return self.buf.at[span, lax.rem(self.x + step, X_CHIPS), core, 1]

    def both_ways(self, ref, half, first, s, r):
        self.send(ref, ref, s(0), r(0), self.near(half, 1, first))
        self.send(ref, ref, s(1), r(1), self.near(half, 3, first))

    def start(self, half):
        s, r = (lambda i: self.s1.at[half, i]), (lambda i: self.r1.at[half, i])
        self.both_ways(self.block(half, 0), half, True, s, r)

    def relay(self, half):
        ref = self.block(half, 3 + 2 * self.core)
        arrived(ref, self.r1.at[half, self.core])
        to = self.near(half, 1 + 2 * self.core, True)
        self.send(ref, ref, self.s1.at[half, 2], self.r1.at[half, 2], to)

    def turn(self, half):
        arrived(self.block(half, 1 + 2 * self.core), self.r1.at[half, 1 - self.core])
        arrived(self.block(half, 2), self.r1.at[half, 2])
        for pair in range(2):
            s, r = (lambda i: self.s2.at[half, pair, i]), (lambda i: self.r2.at[half, pair, i])
            self.both_ways(self.line(half, 0, pair), half, False, s, r)
        self.share(half, 0)

    def share(self, half, step):
        ref = self.line(half, step)
        to = place(self.y, self.x, 1 - self.core)
        self.send(ref, ref, self.sc.at[half, step], self.rc.at[half, step], to)

    def relay_line(self, half, pair):
        ref = self.line(half, 3 + 2 * self.core, pair)
        arrived(ref, self.r2.at[half, pair, self.core])
        to = self.near(half, 1 + 2 * self.core, False)
        self.send(ref, ref, self.s2.at[half, pair, 2], self.r2.at[half, pair, 2], to)

    def sides(self, half):
        for pair in range(2):
            ref = self.line(half, 1 + 2 * self.core, pair)
            arrived(ref, self.r2.at[half, pair, 1 - self.core])
        self.share(half, 3)
        self.share(half, 1)

    def far(self, half):
        for pair in range(2):
            arrived(self.line(half, 2, pair), self.r2.at[half, pair, 2])
        self.share(half, 2)

    def shared(self, half, step):
        arrived(self.line(half, step, other=True), self.rc.at[half, step])


def mixer_kernel(
    acts,
    gains,
    w_kv,
    dt_in_any,
    dt_out_any,
    dt_bias,
    decay_rate,
    w_bc_any,
    skip_gain,
    w_router_any,
    routes,
    packed,
    weighting,
    second,
    weights,
    kv,
    normed,
    queries,
    largest,
    total,
    summed,
    first,
    mixed,
    keep,
    drive,
    both_vmem,
    both,
    message,
    inbox,
    outbox,
    incoming,
    dt_in,
    dt_out,
    w_bc,
    w_router,
    load_sem,
    scan_send,
    scan_recv,
    w_s1,
    w_r1,
    w_s2,
    w_r2,
    w_sc,
    w_rc,
    kv_s1,
    kv_r1,
    kv_s2,
    kv_r2,
    kv_sc,
    kv_rc,
):
    y, x, core = coordinates()
    ctx = lax.axis_index("ctx")
    devices = 2 * X_CHIPS * Y_CHIPS
    rows, width = acts.shape
    lanes = 128
    blocks = width // lanes
    f32, bf16 = jnp.float32, jnp.bfloat16
    loads = [
        pltpu.make_async_copy(src, dst, load_sem.at[i])
        for i, (src, dst) in enumerate(
            [(dt_in_any, dt_in), (dt_out_any, dt_out), (w_bc_any, w_bc), (w_router_any, w_router)]
        )
    ]
    for load in loads:
        load.start()
    barrier = pltpu.get_barrier_semaphore()

    def hail(step, carry):
        peer = {"ctx": lax.rem(ctx + step, devices)}
        pl.semaphore_signal(barrier, inc=1, device_id=peer, device_id_type=pl.DeviceIdType.MESH)
        return carry

    lax.fori_loop(1, devices, hail, 0)
    send = Sender()

    for half in range(2):
        weights[y, x, core, half] = w_kv[half * 16 : half * 16 + 16]
    normed[...] = rms_norm(acts[...].astype(f32), gains[0:1]).astype(bf16)
    for head in range(HEADS):
        group, place_in = divmod(head, HEADS // KVH)
        queries[group, place_in * rows : (place_in + 1) * rows] = normed[:, head * HD : (head + 1) * HD]
    pl.semaphore_wait(barrier, devices - 1)
    w_gather = Gather(weights, (w_s1, w_r1, w_s2, w_r2, w_sc, w_rc), send)
    for step in (w_gather.start, w_gather.relay, w_gather.turn):
        for half in range(2):
            step(half)
    for pair in range(2):
        for half in range(2):
            w_gather.relay_line(half, pair)
    for step in (w_gather.sides, w_gather.far):
        for half in range(2):
            step(half)
    for half in range(2):
        for step in range(4):
            w_gather.shared(half, step)

    for part in range(4):
        made = lax.dot_general(
            normed[...],
            weights[part].reshape(2 * HD, width),
            (((1,), (1,)), ((), ())),
            preferred_element_type=f32,
        ).astype(bf16)
        for head in range(2):
            kv[y, x, core, part % 2, part // 2 * 2 + head] = made[:, head * HD : (head + 1) * HD]

    kv_gather = Gather(kv, (kv_s1, kv_r1, kv_s2, kv_r2, kv_sc, kv_rc), send)
    for step in (kv_gather.start, kv_gather.relay, kv_gather.turn):
        for half in range(2):
            step(half)
    group = HEADS // KVH
    keys_here = 2 * X_CHIPS * rows
    queue = lax.broadcasted_iota(jnp.int32, (group, rows, 1), 1).reshape(group * rows, 1) + ctx * rows
    column = lax.broadcasted_iota(jnp.int32, (1, keys_here), 1)

    def attend(half, step):
        kv_gather.shared(half, step)
        if half == 0:
            line = lax.rem(y + step, Y_CHIPS)
            key_pos = column + line * keys_here
        else:
            line = lax.rem(x + step, X_CHIPS)
            per_chip = 2 * rows
            key_pos = column // per_chip * keys_here + line * per_chip + column % per_chip
        allowed = key_pos <= queue

        def one_head(head, carry):
            g = 2 * half + head
            if half == 0:
                k, v = kv[line, :, :, 0, head], kv[line, :, :, 0, 2 + head]
            else:
                k, v = kv[:, line, :, 1, head], kv[:, line, :, 1, 2 + head]
            k, v = k.reshape(keys_here, HD), v.reshape(keys_here, HD)
            scores = lax.dot_general(
                queries[g], k, (((1,), (1,)), ((), ())), preferred_element_type=f32
            ) * (HD**-0.5 * LOG2E)
            scores = jnp.where(allowed, scores, -1e30)
            top = jnp.max(scores, -1, keepdims=True)
            if step == 0:
                newest = jnp.broadcast_to(top, (group * rows, lanes))
            else:
                newest = jnp.maximum(largest[g], top)
            wide = jnp.concatenate([newest] * (keys_here // lanes), 1)
            probs = jnp.exp2(scores - wide)
            sums = jnp.sum(probs, -1, keepdims=True)
            mixed_in = jnp.dot(probs.astype(bf16), v, preferred_element_type=f32)
            if step == 0:
                total[g] = jnp.broadcast_to(sums, (group * rows, lanes))
                summed[g] = mixed_in
            else:
                fade = jnp.exp2(largest[g] - newest)
                total[g] = total[g] * fade + sums
                summed[g] = summed[g] * fade + mixed_in
            largest[g] = newest
            return carry

        lax.fori_loop(0, 2, one_head, 0)

    for half in range(2):
        attend(half, 0)
    for pair in range(2):
        for half in range(2):
            kv_gather.relay_line(half, pair)
    for half in range(2):
        kv_gather.sides(half)
    for half in range(2):
        for step in (3, 1):
            attend(half, step)
    for half in range(2):
        kv_gather.far(half)
    for half in range(2):
        attend(half, 2)

    for head in range(HEADS):
        g, r = divmod(head, group)
        span = slice(head * HD, (head + 1) * HD)
        here = slice(r * rows, (r + 1) * rows)
        first[:, span] = acts[:, span].astype(f32) + summed[g, here] / total[g, here]

    mixed[...] = rms_norm(first[...], gains[1:2]).astype(bf16)
    for load in loads:
        load.wait()
    both_vmem[:, 0:32] = jnp.dot(mixed[...], w_bc[...], preferred_element_type=f32)
    to_scalars = pltpu.make_async_copy(both_vmem, both, load_sem.at[0])
    to_scalars.start()
    low_rank = jnp.dot(mixed[...], dt_in[...], preferred_element_type=f32).astype(bf16)
    for i in range(blocks):
        span = slice(i * lanes, (i + 1) * lanes)
        raw = jnp.dot(low_rank, dt_out[:, span], preferred_element_type=f32) + dt_bias[:, span]
        step_size = jnp.maximum(raw, 0.0) + jnp.log1p(jnp.exp(-jnp.abs(raw)))
        keep[:, i, :] = jnp.exp(-step_size * decay_rate[:, span])
        drive[:, i, :] = step_size * mixed[:, span].astype(f32)
    to_scalars.wait()
    states = 16

    def advance(t, carry):
        state, product = carry
        kept, driven = keep[t], drive[t]
        state = tuple(s * kept + driven * both[t, n] for n, s in enumerate(state))
        terms = [s * both[t, states + n] for n, s in enumerate(state)]
        while len(terms) > 1:
            terms = [a + b for a, b in zip(terms[::2], terms[1::2])]
        product = product * kept
        drive[t] = terms[0]
        keep[t] = product
        return state, product

    zero = jnp.zeros((blocks, lanes), f32)
    state, product = lax.fori_loop(
        0, rows, advance, ((zero,) * states, jnp.ones((blocks, lanes), f32))
    )

    for n in range(states):
        for part in range(2):
            message[2 * n + part, 0] = state[n][part * 8 : part * 8 + 8]
            message[2 * n + part, 1] = product[part * 8 : part * 8 + 8]

    def swap(count, mine, theirs, semaphore):
        own = pltpu.make_async_copy(mine(ctx), theirs(ctx), scan_recv.at[semaphore])
        own.start()

        def one(step, carry):
            peer = lax.rem(ctx + step, devices)
            pltpu.make_async_remote_copy(
                src_ref=mine(peer),
                dst_ref=theirs(ctx),
                send_sem=scan_send.at[semaphore],
                recv_sem=scan_recv.at[semaphore],
                device_id={"ctx": peer},
                device_id_type=pl.DeviceIdType.MESH,
            ).start()
            return carry

        lax.fori_loop(1, devices, one, 0)

    swap(0, lambda j: message.at[j], lambda j: inbox.at[j], 0)
    arrived(inbox, scan_recv.at[0])

    def join(turn, entering):
        outbox[turn] = entering
        return inbox[turn, 1] * entering + inbox[turn, 0]

    lax.fori_loop(0, devices, join, jnp.zeros((8, lanes), f32))

    def slot(j):
        return incoming.at[lax.div(j, 2), pl.ds(pl.multiple_of(lax.rem(j, 2) * 8, 8), 8)]

    swap(0, lambda j: outbox.at[j], slot, 1)
    arrived(incoming, scan_recv.at[1])

    def carry_in(t, held):
        terms = [s * both[t, states + n] for n, s in enumerate(held)]
        while len(terms) > 1:
            terms = [a + b for a, b in zip(terms[::2], terms[1::2])]
        drive[t] = drive[t] + keep[t] * terms[0]
        return held

    lax.fori_loop(0, rows, carry_in, tuple(incoming[n] for n in range(states)))
    for i in range(blocks):
        span = slice(i * lanes, (i + 1) * lanes)
        second[:, span] = (
            first[:, span] + drive[:, i, :] + skip_gain[:, span] * mixed[:, span].astype(f32)
        )

    normed[...] = rms_norm(second[...], gains[2:3]).astype(bf16)
    logits = jnp.dot(normed[...], w_router[...], preferred_element_type=f32)
    expert = lax.broadcasted_iota(jnp.int32, (rows, EXPERTS), 1)
    hits = [(routes[:, i : i + 1] == expert).astype(f32) for i in range(2)]
    chosen = [jnp.sum(hit * logits, -1, keepdims=True) for hit in hits]
    top = jnp.maximum(chosen[0], chosen[1])
    powers = [jnp.exp(c - top) for c in chosen]
    share = powers[0] + powers[1]
    gates = hits[0] * (powers[0] / share) + hits[1] * (powers[1] / share)
    hit = hits[0] + hits[1]
    row_at = lax.broadcasted_iota(jnp.int32, (rows, rows), 0)
    col_at = lax.broadcasted_iota(jnp.int32, (rows, rows), 1)
    earlier = (col_at < row_at).astype(bf16)
    rank = jnp.dot(earlier, hit.astype(bf16), preferred_element_type=f32)
    capacity = packed.shape[1]
    slots = lax.broadcasted_iota(jnp.int32, (rows, EXPERTS * capacity), 1).astype(f32)
    placing = jnp.zeros(slots.shape, f32)
    gate = jnp.zeros(slots.shape, f32)
    for e in range(EXPERTS):
        here = (slots == rank[:, e : e + 1] + e * capacity).astype(f32) * hit[:, e : e + 1]
        placing = placing + here
        gate = gate + here * gates[:, e : e + 1]
    weighting[...] = gate
    placing = placing.astype(bf16)
    for j in range(4):
        span = slice(j * width // 4, (j + 1) * width // 4)
        packed[:, :, span] = (
            lax.dot_general(
                placing, normed[:, span], (((0,), (0,)), ((), ())), preferred_element_type=f32
            )
            .astype(bf16)
            .reshape(EXPERTS, capacity, width // 4)
        )
    send.finish()
    sent = inbox.at[pl.ds(0, devices - 1)]
    arrived(sent, scan_send.at[0])
    sent = outbox.at[pl.ds(0, devices - 1)]
    arrived(sent, scan_send.at[1])


def mixer(acts, gains, w_kv, dt_in, dt_out, dt_bias, decay_rate, w_bc, skip_gain, w_router, routes):
    rows, width = acts.shape
    f32, bf16 = jnp.float32, jnp.bfloat16
    dma = pltpu.SemaphoreType.DMA
    whole = pl.BlockSpec(memory_space=pltpu.VMEM)
    apart = pl.BlockSpec(memory_space=pl.ANY)
    capacity = rows * routes.shape[1] // EXPERTS
    grid = (Y_CHIPS, X_CHIPS, 2, 2)
    devices = 2 * X_CHIPS * Y_CHIPS
    blocks = width // 128
    queries = (KVH, HEADS // KVH * rows, HD)
    gather_sems = [dma((2, 3)), dma((2, 3)), dma((2, 2, 3)), dma((2, 2, 3)), dma((2, 4)), dma((2, 4))]
    return pl.pallas_call(
        mixer_kernel,
        out_shape=(
            jax.ShapeDtypeStruct((EXPERTS, capacity, width), bf16),
            jax.ShapeDtypeStruct((rows, EXPERTS * capacity), f32),
            jax.ShapeDtypeStruct((rows, width), f32),
        ),
        in_specs=[whole, whole, whole, apart, apart, whole, whole, apart, whole, apart, whole],
        out_specs=(whole, whole, whole),
        scratch_shapes=[
            pltpu.VMEM(grid + (16, width), bf16),
            pltpu.VMEM(grid + (4, rows, HD), bf16),
            pltpu.VMEM((rows, width), bf16),
            pltpu.VMEM(queries, bf16),
            pltpu.VMEM(queries, f32),
            pltpu.VMEM(queries, f32),
            pltpu.VMEM(queries, f32),
            pltpu.VMEM((rows, width), f32),
            pltpu.VMEM((rows, width), bf16),
            pltpu.VMEM((rows, blocks, 128), f32),
            pltpu.VMEM((rows, blocks, 128), f32),
            pltpu.VMEM((rows, 128), f32),
            pltpu.SMEM((rows, 128), f32),
            pltpu.VMEM((devices, 2, 8, 128), f32),
            pltpu.VMEM((devices, 2, 8, 128), f32),
            pltpu.VMEM((devices, 8, 128), f32),
            pltpu.VMEM((16, blocks, 128), f32),
            pltpu.VMEM(dt_in.shape, bf16),
            pltpu.VMEM(dt_out.shape, bf16),
            pltpu.VMEM(w_bc.shape, bf16),
            pltpu.VMEM(w_router.shape, bf16),
            dma((4,)),
            dma((2,)),
            dma((2,)),
        ]
        + gather_sems
        + gather_sems,
        compiler_params=pltpu.CompilerParams(
            collective_id=2, has_side_effects=True, vmem_limit_bytes=48 * MIB
        ),
        name="mixer",
    )(acts, gains, w_kv, dt_in, dt_out, dt_bias, decay_rate, w_bc, skip_gain, w_router, routes)


def moe_kernel(
    packed,
    weighting,
    second,
    up_any,
    down_any,
    handed,
    out,
    finished,
    rows,
    parts,
    sibling_parts,
    far_parts,
    side_parts,
    up,
    down,
    hidden,
    weight_sem,
    send_y,
    recv_y,
    send_side,
    recv_side,
    send_far,
    recv_far,
    send_core,
    recv_core,
    back_core_send,
    back_core_recv,
    back_far_send,
    back_far_recv,
    back_side_send,
    back_side_recv,
    back_y_send,
    back_y_recv,
    hand_send,
    hand_recv,
):
    y, x, core = coordinates()
    left = lax.rem(x + X_CHIPS - 1, X_CHIPS)
    right = lax.rem(x + 1, X_CHIPS)
    far = lax.rem(x + 2, X_CHIPS)
    chips = (x, left, right, far)
    on_left, on_right, on_core = place(y, left, core), place(y, right, core), place(y, x, 1 - core)
    send = Sender()

    def row_of(k):
        return lax.rem(y + k, Y_CHIPS)

    load_up = pltpu.make_async_copy(up_any, up, weight_sem.at[0])
    load_down = pltpu.make_async_copy(down_any, down, weight_sem.at[1])
    load_up.start()
    load_down.start()
    segment, segments = lax.axis_index("segment"), lax.axis_size("segment")
    ahead = {"segment": lax.rem(segment + 1, segments)}
    behind = {"segment": lax.rem(segment + segments - 1, segments)}
    peers = [on_left, on_right, on_core] + [place(row_of(k), x, core) for k in (1, 2, 3)]
    peers = peers + [ahead, behind]
    greet(peers)
    greeted(len(peers))

    def block(at, k):
        return rows.at[chips[at], core, row_of(k)]

    def own_block(k):
        send(block(0, k), block(0, k), send_side.at[0, k], recv_side.at[0, k], on_right)
        send(block(0, k), block(0, k), send_side.at[1, k], recv_side.at[1, k], on_left)
        send(block(0, k), block(0, k), send_core.at[0, k], recv_core.at[0, k], on_core)

    def side_block(k):
        arrived(block(1, k), recv_side.at[0, k])
        if k in (0, 1):
            send(block(1, k), block(1, k), send_far.at[k], recv_far.at[k], on_right)
        send(block(1, k), block(1, k), send_core.at[1, k], recv_core.at[1, k], on_core)
        arrived(block(2, k), recv_side.at[1, k])
        if k in (2, 3):
            send(block(2, k), block(2, k), send_far.at[k], recv_far.at[k], on_left)
        send(block(2, k), block(2, k), send_core.at[2, k], recv_core.at[2, k], on_core)

    def far_block(k):
        arrived(block(3, k), recv_far.at[k])
        send(block(3, k), block(3, k), send_core.at[3, k], recv_core.at[3, k], on_core)

    def from_core(at):
        for k in range(Y_CHIPS):
            other = rows.at[chips[at], 1 - core, row_of(k)]
            arrived(other, recv_core.at[at, k])

    def experts(at):
        chip = chips[at]

        def one_core(turn, carry):
            which = lax.rem(1 - core + turn, 2)
            taken = rows[chip, which].reshape(-1, rows.shape[-1])
            lifted = jnp.dot(taken, up[...], preferred_element_type=jnp.float32)
            hidden[...] = jax.nn.silu(lifted).astype(jnp.bfloat16)

            def columns(j, carry):
                span = pl.ds(pl.multiple_of(j * 512, 512), 512)
                lowered = jnp.dot(hidden[...], down[:, span], preferred_element_type=jnp.float32)
                parts[chip, which, :, :, span] = lowered.astype(jnp.bfloat16).reshape(
                    Y_CHIPS, -1, 512
                )
                return carry

            return lax.fori_loop(0, rows.shape[-1] // 512, columns, carry)

        lax.fori_loop(0, 2, one_core, 0)
        send(
            parts.at[chip, 1 - core],
            sibling_parts.at[chip],
            back_core_send.at[at],
            back_core_recv.at[at],
            on_core,
        )

    def added(*refs):
        total = refs[0][...].astype(jnp.float32)
        for ref in refs[1:]:
            total = total + ref[...].astype(jnp.float32)
        return total.astype(jnp.bfloat16)

    def mine(at, k):
        return parts.at[chips[at], core, row_of(k)]

    def theirs(at, k):
        return sibling_parts.at[chips[at], row_of(k)]

    for k in (1, 3, 2):
        send(
            packed.at[row_of(k)],
            rows.at[x, core, y],
            send_y.at[k],
            recv_y.at[4 - k],
            place(row_of(k), x, core),
        )
    rows[x, core, y] = packed[y]
    own_block(0)
    for k in (1, 3, 2):
        arrived(block(0, k), recv_y.at[k])
        own_block(k)
    load_up.wait()
    load_down.wait()
    from_core(0)
    side_block(0)
    experts(0)
    for k in (1, 3, 2):
        side_block(k)
    from_core(1)
    experts(1)
    far_block(0)
    from_core(2)
    experts(2)
    for k in (1, 3, 2):
        far_block(k)

    def core_sum(at):
        arrived(sibling_parts.at[chips[at]], back_core_recv.at[at])

    def to_side(at, k, relayed):
        if relayed:
            slot = far_parts.at[k]
            arrived(slot, back_far_recv.at[k])
            mine(at, k)[...] = added(mine(at, k), theirs(at, k), slot)
        else:
            mine(at, k)[...] = added(mine(at, k), theirs(at, k))
        to = on_left if at == 1 else on_right
        send(
            mine(at, k),
            side_parts.at[at - 1, k],
            back_side_send.at[at - 1, k],
            back_side_recv.at[at - 1, k],
            to,
        )

    core_sum(1)
    core_sum(2)
    for k in (3, 0):
        to_side(1, k, False)
    for k in (2, 1):
        to_side(2, k, False)
    from_core(3)
    experts(3)
    core_sum(3)
    for k in (2, 3, 1, 0):
        mine(3, k)[...] = added(mine(3, k), theirs(3, k))
        to = on_left if k in (2, 1) else on_right
        send(mine(3, k), far_parts.at[k], back_far_send.at[k], back_far_recv.at[k], to)
    core_sum(0)
    for k in (2, 3, 1, 0):
        to_side(1 if k in (2, 1) else 2, k, True)
    for k in (2, 3, 1, 0):
        for at in (1, 2):
            arrived(side_parts.at[at - 1, k], back_side_recv.at[at - 1, k])
        total = added(mine(0, k), theirs(0, k), side_parts.at[0, k], side_parts.at[1, k])
        if k == 0:
            out[y] = total
        else:
            mine(0, k)[...] = total
            send(
                mine(0, k),
                out.at[y],
                back_y_send.at[k],
                back_y_recv.at[4 - k],
                place(row_of(k), x, core),
            )
    for k in (1, 3, 2):
        arrived(out.at[row_of(k)], back_y_recv.at[k])
    gate = weighting[...]
    high = gate.astype(jnp.bfloat16)
    low = (gate - high.astype(jnp.float32)).astype(jnp.bfloat16)
    strip = 512
    for j in range(rows.shape[-1] // strip):
        span = pl.ds(j * strip, strip)
        expert_out = out[:, :, span].reshape(-1, strip)
        mixture_rows = jnp.dot(high, expert_out, preferred_element_type=jnp.float32) + jnp.dot(
            low, expert_out, preferred_element_type=jnp.float32
        )
        finished[:, span] = (second[:, span] + mixture_rows).astype(jnp.bfloat16)
        send(finished.at[:, span], handed.at[:, span], hand_send.at[j], hand_recv.at[j], ahead)
    for j in range(rows.shape[-1] // strip):
        arrived(handed.at[:, pl.ds(j * strip, strip)], hand_recv.at[j])
    send.finish()


def mixture(packed, weighting, second, w_up, w_down):
    experts, capacity, width = packed.shape
    units = w_up.shape[1]
    kind = jnp.bfloat16
    block = (capacity, width)
    dma = pltpu.SemaphoreType.DMA
    return pl.pallas_call(
        moe_kernel,
        out_shape=jax.ShapeDtypeStruct(second.shape, kind),
        in_specs=[
            pl.BlockSpec(memory_space=pltpu.VMEM),
            pl.BlockSpec(memory_space=pltpu.VMEM),
            pl.BlockSpec(memory_space=pltpu.VMEM),
            pl.BlockSpec(memory_space=pl.ANY),
            pl.BlockSpec(memory_space=pl.ANY),
        ],
        out_specs=pl.BlockSpec(memory_space=pltpu.VMEM),
        scratch_shapes=[
            pltpu.VMEM(packed.shape, kind),
            pltpu.VMEM(second.shape, kind),
            pltpu.VMEM((X_CHIPS, 2, Y_CHIPS) + block, kind),
            pltpu.VMEM((X_CHIPS, 2, Y_CHIPS) + block, kind),
            pltpu.VMEM((X_CHIPS, Y_CHIPS) + block, kind),
            pltpu.VMEM((Y_CHIPS,) + block, kind),
            pltpu.VMEM((2, Y_CHIPS) + block, kind),
            pltpu.VMEM(w_up.shape, kind),
            pltpu.VMEM(w_down.shape, kind),
            pltpu.VMEM((Y_CHIPS * capacity, units), kind),
            dma((2,)),
            dma((4,)),
            dma((4,)),
            dma((2, 4)),
            dma((2, 4)),
            dma((4,)),
            dma((4,)),
            dma((4, 4)),
            dma((4, 4)),
            dma((4,)),
            dma((4,)),
            dma((4,)),
            dma((4,)),
            dma((2, 4)),
            dma((2, 4)),
            dma((4,)),
            dma((4,)),
            dma((4,)),
            dma((4,)),
        ],
        compiler_params=pltpu.CompilerParams(
            collective_id=1, has_side_effects=True, vmem_limit_bytes=56 * MIB
        ),
        name="mixture",
    )(packed, weighting, second, w_up, w_down)


def on_device(
    acts,
    norm_gains,
    w_kv,
    dt_in,
    dt_out,
    dt_bias,
    decay_rate,
    w_bc,
    skip_gain,
    w_router,
    routes,
    w_up,
    w_down,
):
    packed, weighting, second = mixer(
        acts[0],
        norm_gains[0],
        w_kv[0].T,
        dt_in[0],
        dt_out[0],
        dt_bias,
        decay_rate,
        w_bc[0],
        skip_gain,
        w_router[0],
        routes[0],
    )
    return mixture(packed, weighting, second, w_up[0], w_down[0])[None]


def solution(mesh):
    in_specs = (
        P("segment", "ctx", None),
        P("segment", None, None),
        P("segment", None, "ctx"),
        P("segment", None, None),
        P("segment", None, None),
        P("segment", None),
        P("segment", None),
        P("segment", None, None),
        P("segment", None),
        P("segment", None, None),
        P("segment", "ctx", None),
        P("segment", None, "ctx"),
        P("segment", "ctx", None),
    )
    out_specs = P("segment", "ctx", None)
    return jax.shard_map(
        on_device, mesh=mesh, in_specs=in_specs, out_specs=out_specs, check_vma=False
    )
```

time: 438 us -> 217 us (0.50)
  waiting for transfers between devices: 165 us -> 0 us
  Pallas kernels: 119 us -> 201 us
  matrix products: 60.1 us -> 0 us
  other arithmetic: 36.3 us -> 0 us
  blocking collectives: 24 us -> 0 us
  between operations: 13.5 us -> 0.06 us
    all_gather x4 -> x0, waiting for transfers between devices: 151 us -> none  [the longest x1 56 us: on_device(): lax.all_gather(w_kv[0], 'ctx', axis=1, tiled=True)]
    pallas_call x1 -> x2, Pallas kernels: 119 us -> 201 us  [the longest x1 109 us: mixture(): pl.pallas_call(moe_kernel, out_shape=jax.ShapeDtypeStruct(second.shape, k...]
    dot_general x25 -> x0, matrix products: 60.1 us -> none  [the longest x1 16.8 us: on_device(): jnp.einsum('tgrs,sgd->tgrd', weights.astype(jnp.bfloat16), value_piece, p...]
    reduce_sum x9 -> x0, other arithmetic: 26.7 us -> none  [the longest x1 14.7 us: on_device(): total = jnp.sum(weights, -1)]
    all_gather x1 -> x0, blocking collectives: 24 us -> none  [entering(): lax.all_gather(a.astype(kind), axis)]
    ppermute x1 -> x0, waiting for transfers between devices: 13.7 us -> none  [shifted(): return lax.ppermute(value, axis, pairs)]
    unnamed x18 -> x25, local copies, waits for them, and re-layouts: 0.95 us -> 14.4 us
    reshape x6 -> x0, local copies, waits for them, and re-layouts: 4.63 us -> none  [the longest x1 1.56 us: on_device(): first = start_x + (summed / total[..., None]).reshape(rows_here, width)]
  transfers between devices with their start and end apart: 5 -> 0, of which waited for: 5 -> 0; matrix products, arithmetic and copies ran while one was open for 9% -> 0% of each run, Pallas kernels for 0% -> 0%
where the time goes in v2:
time: 217 us; the launch traced here: 216 us
  Pallas kernels  201 us (93%)
  local copies, waits for them, and re-layouts  14.4 us (7%)
    pallas_call x1, Pallas kernels, mixture(): pl.pallas_call(moe_kernel, out_shape=jax.ShapeDtypeStruct(second.shape, k...  109 us
    pallas_call x1, Pallas kernels, mixer(): pl.pallas_call(mixer_kernel, out_shape=(jax.ShapeDtypeStruct((EXPERTS, ca...  92.4 us
    unnamed x25, local copies, waits for them, and re-layouts  14.4 us

profile of v2, /device:TPU:1, one launch (start us, length us, event | category | flops | bytes accessed | tf_op | source)
XLA Modules:
  0.0 215.7 jit_solution(14006032752710235423)
XLA Ops:
  0.0 0.8 copy.19
  0.8 0.8 copy.16
  1.5 1.2 copy.14
  2.7 1.0 copy.15
  3.8 0.0 copy-start.2
  3.8 1.0 copy-done.2
  4.8 0.0 copy-start.3
  4.8 1.0 copy-done.3
  5.8 0.0 copy-start.4
  5.9 1.0 copy-done.4
  6.9 0.0 copy-start.6
  6.9 0.9 copy-done.6
  7.8 0.0 copy-start.7
  7.8 0.7 copy-done.7
  8.5 0.0 copy-start.8
  8.5 0.7 copy-done.8
  9.2 0.7 copy-done.9
  9.9 92.4 %mixer.1 = (bf16[4,64,2048]{2,1,0:T(8,128)(2,1)S(1)}, f32[128,256]{1,0:T(8,128)S(1)}, f32[128,2048]{1,0:T(8,128)S(1)}) custom-call(bf16[128,2048]{1,0:T(8,128)(2,1)S(1)} %bitcast.17, f32[3,2048]{1,0:T(4,128)S(1)} %bitcast.21, bf16[32,2048]{1,0:T(8,128)(2,1)S(1)} %bitcast.22, bf16[2048,128]{1,0:T(8,128)(2,1)S(1)} %bitcast.18, bf16[128,2048]{1,0:T(8,128)(2,1)S(1)} %bitcast.19, ...), custom_call_target="tpu_custom_call" | custom-call | tf_op jit(solution)/shard_map/mixer/pallas_call | solution.py:457
  102.3 0.0 copy-start
  102.3 1.0 copy-done
  103.3 1.0 copy-done.1
  104.3 0.7 copy-done.5
  104.9 108.9 %mixture.1 = bf16[128,2048]{1,0:T(8,128)(2,1)} custom-call(bf16[4,64,2048]{2,1,0:T(8,128)(2,1)} %copy-done, f32[128,256]{1,0:T(8,128)} %copy-done.5, f32[128,2048]{1,0:T(8,128)} %copy-done.1, bf16[2048,896]{1,0:T(8,128)(2,1)} %bitcast.23, bf16[896,2048]{1,0:T(8,128)(2,1)} %bitcast.24), custom_call_target="tpu_custom_call" | custom-call | tf_op jit(solution)/shard_map/mixture/pallas_call | solution.py:731
  213.8 1.9 copy.21
  (3 shorter events, 0.0 us)
Async XLA Ops:
  3.8 1.0 copy-start.2
  4.8 1.0 copy-start.3
  5.8 1.0 copy-start.4
  6.9 0.9 copy-start.6
  7.8 0.7 copy-start.7
  8.5 0.7 copy-start.8
  9.2 0.7 copy-start.9
  102.3 1.0 copy-start
  103.3 1.0 copy-start.1
  104.3 0.7 copy-start.5

commit v3 on v0

v3 whole, which is shorter than its diff:
```python
import functools

import jax
import jax.numpy as jnp
from jax import lax
from jax.experimental import pallas as pl
from jax.experimental.pallas import tpu as pltpu
from jax.sharding import PartitionSpec as P

HEADS = 16
KVH = 4
HD = 128
EXPERTS = 4
X_CHIPS = 4
Y_CHIPS = 4
MIB = 1 << 20
LOG2E = 1.4426950408889634


def place(y, x, core):
    return {"ctx": (y * X_CHIPS + x) * 2 + core}


def coordinates():
    ctx = lax.axis_index("ctx")
    return lax.div(ctx, 2 * X_CHIPS), lax.rem(lax.div(ctx, 2), X_CHIPS), lax.rem(ctx, 2)


def arrived(dst, sem):
    pltpu.make_async_copy(dst, dst, sem).wait()


def rms_norm(values, gain):
    return values * lax.rsqrt(jnp.mean(values * values, -1, keepdims=True) + 1e-06) * gain


class Sender:
    def __init__(self):
        self.started = []

    def __call__(self, src, dst, send_sem, recv_sem, to):
        copy = pltpu.make_async_remote_copy(
            src_ref=src,
            dst_ref=dst,
            send_sem=send_sem,
            recv_sem=recv_sem,
            device_id=to,
            device_id_type=pl.DeviceIdType.MESH,
        )
        copy.start()
        self.started.append(copy)

    def both_ways(self, ref, sends, receives, ahead, behind):
        self(ref, ref, sends(0), receives(0), ahead)
        self(ref, ref, sends(1), receives(1), behind)

    def finish(self):
        for copy in self.started:
            copy.wait_send()


class Gather:
    def __init__(self, buf, sems, send):
        self.buf, self.send = buf, send
        self.s1, self.r1, self.s2, self.r2, self.sc, self.rc = sems
        self.y, self.x, self.core = coordinates()
        self.behind, self.ahead = lax.rem(3 + 2 * self.core, 4), lax.rem(1 + 2 * self.core, 4)

    def near(self, half, step, first):
        along_x = (half == 0) == first
        if along_x:
            return place(self.y, lax.rem(self.x + step, X_CHIPS), self.core)
        return place(lax.rem(self.y + step, Y_CHIPS), self.x, self.core)

    def block(self, half, step, item):
        if half == 0:
            return self.buf.at[lax.rem(self.y + step, Y_CHIPS), lax.rem(self.x + item, X_CHIPS), self.core, 0]
        return self.buf.at[lax.rem(self.y + item, Y_CHIPS), lax.rem(self.x + step, X_CHIPS), self.core, 1]

    def line(self, half, step, other=False):
        core = 1 - self.core if other else self.core
        if half == 0:
            return self.buf.at[lax.rem(self.y + step, Y_CHIPS), :, core, 0]
        return self.buf.at[:, lax.rem(self.x + step, X_CHIPS), core, 1]

    def spread(self, half, item):
        self.send.both_ways(
            self.block(half, 0, item),
            lambda i: self.s2.at[half, item, i],
            lambda i: self.r2.at[half, item, i],
            self.near(half, 1, False),
            self.near(half, 3, False),
        )

    def start(self, half):
        self.send.both_ways(
            self.block(half, 0, 0),
            lambda i: self.s1.at[half, i],
            lambda i: self.r1.at[half, i],
            self.near(half, 1, True),
            self.near(half, 3, True),
        )

    def relay(self, half):
        ref = self.block(half, 0, self.behind)
        arrived(ref, self.r1.at[half, self.core])
        to = self.near(half, self.ahead, True)
        self.send(ref, ref, self.s1.at[half, 2], self.r1.at[half, 2], to)
        self.spread(half, self.behind)

    def turn(self, half):
        arrived(self.block(half, 0, self.ahead), self.r1.at[half, 1 - self.core])
        self.spread(half, self.ahead)

    def turn_far(self, half):
        arrived(self.block(half, 0, 2), self.r1.at[half, 2])
        self.spread(half, 2)
        self.share(half, 0)

    def share(self, half, step):
        ref = self.line(half, step)
        to = place(self.y, self.x, 1 - self.core)
        self.send(ref, ref, self.sc.at[half, step], self.rc.at[half, step], to)

    def relay_line(self, half, item):
        ref = self.block(half, self.behind, item)
        arrived(ref, self.r2.at[half, item, self.core])
        to = self.near(half, self.ahead, False)
        self.send(ref, ref, self.s2.at[half, item, 2], self.r2.at[half, item, 2], to)

    def sides(self, half):
        for item in (0, self.behind, self.ahead, 2):
            arrived(self.block(half, self.ahead, item), self.r2.at[half, item, 1 - self.core])
        self.share(half, 3)
        self.share(half, 1)

    def far(self, half):
        for item in (0, self.behind, self.ahead, 2):
            arrived(self.block(half, 2, item), self.r2.at[half, item, 2])
        self.share(half, 2)

    def shared(self, half, step):
        arrived(self.line(half, step, other=True), self.rc.at[half, step])

    def begin(self):
        for step in (self.start, lambda half: self.spread(half, 0), self.relay, self.turn, self.turn_far):
            for half in range(2):
                step(half)

    def pass_on(self):
        for item in (0, self.behind, self.ahead, 2):
            for half in range(2):
                self.relay_line(half, item)


def layer_kernel(names, *refs):
    here = dict(zip(names, refs))
    mix(here)
    experts(here)


def mix(ref):
    y, x, core = coordinates()
    ctx = lax.axis_index("ctx")
    devices = 2 * X_CHIPS * Y_CHIPS
    loaded = ("acts", "gains", "w_kv", "dt_bias", "decay_rate", "skip_gain", "routes")
    loaded = loaded + ("dt_in", "dt_out", "w_bc", "w_router", "up", "down")
    loads = {}
    for i, name in enumerate(loaded):
        loads[name] = pltpu.make_async_copy(ref[name + "_any"], ref[name], ref["load_sem"].at[i])
        loads[name].start()
    ref["loads"] = loads
    segment, segments = lax.axis_index("segment"), lax.axis_size("segment")
    barrier = pltpu.get_barrier_semaphore()

    def hail(step, carry):
        peer = {"ctx": lax.rem(ctx + step, devices)}
        pl.semaphore_signal(barrier, inc=1, device_id=peer, device_id_type=pl.DeviceIdType.MESH)
        return carry

    lax.fori_loop(1, devices, hail, 0)
    for step in (1, segments - 1):
        peer = {"segment": lax.rem(segment + step, segments)}
        pl.semaphore_signal(barrier, inc=1, device_id=peer, device_id_type=pl.DeviceIdType.MESH)
    send = ref["send"] = Sender()
    acts, gains, weights, kv = ref["acts"], ref["gains"], ref["weights"], ref["kv"]
    normed, queries, first, mixed = ref["normed"], ref["queries"], ref["first"], ref["mixed"]
    keep, drive, tail = ref["keep"], ref["drive"], ref["tail"]
    both, both_vmem = ref["both"], ref["both_vmem"]
    second, packed, weighting = ref["second"], ref["packed"], ref["weighting"]
    rows, width = acts.shape
    lanes = 128
    blocks = width // lanes
    f32, bf16 = jnp.float32, jnp.bfloat16

    loads["w_kv"].wait()
    for half in range(2):
        weights[y, x, core, half] = ref["w_kv"][half * 16 : half * 16 + 16]
    pl.semaphore_wait(barrier, devices + 1)
    w_gather = Gather(weights, [ref["w_" + name] for name in GATHER_SEMS], Sender())
    w_gather.start(0)
    w_gather.start(1)
    w_gather.spread(0, 0)
    w_gather.spread(1, 0)
    for name in ("acts", "gains"):
        loads[name].wait()
    normed[...] = rms_norm(acts[...].astype(f32), gains[0]).astype(bf16)
    for step in (w_gather.relay, w_gather.turn, w_gather.turn_far):
        for half in range(2):
            step(half)
    for head in range(HEADS):
        group, place_in = divmod(head, HEADS // KVH)
        queries[group, place_in * rows : (place_in + 1) * rows] = normed[:, head * HD : (head + 1) * HD]
    w_gather.pass_on()
    for step in (w_gather.sides, w_gather.far):
        for half in range(2):
            step(half)
    for half in range(2):
        for step in (0, 3, 1, 2):
            w_gather.shared(half, step)

    for part in range(4):
        made = lax.dot_general(
            normed[...],
            weights[part].reshape(2 * HD, width),
            (((1,), (1,)), ((), ())),
            preferred_element_type=f32,
        ).astype(bf16)
        for head in range(2):
            kv[y, x, core, part % 2, part // 2 * 2 + head] = made[:, head * HD : (head + 1) * HD]

    kv_gather = Gather(kv, [ref["kv_" + name] for name in GATHER_SEMS], send)
    kv_gather.begin()
    group = HEADS // KVH
    keys_here = 2 * X_CHIPS * rows
    queue = lax.broadcasted_iota(jnp.int32, (group, rows, 1), 1).reshape(group * rows, 1) + ctx * rows
    column = lax.broadcasted_iota(jnp.int32, (1, keys_here), 1)

    largest, total, summed = keep, drive, tail

    def of(g):
        return pl.ds(g * (group * rows // blocks), group * rows // blocks)

    def stacked(values):
        return values.reshape(group * rows // blocks, blocks, lanes)

    def attend(half, step):
        kv_gather.shared(half, step)
        if half == 0:
            line = lax.rem(y + step, Y_CHIPS)
            key_pos = column + line * keys_here
        else:
            line = lax.rem(x + step, X_CHIPS)
            per_chip = 2 * rows
            key_pos = column // per_chip * keys_here + line * per_chip + column % per_chip
        allowed = key_pos <= queue

        def one_head(head, carry):
            g = 2 * half + head
            if half == 0:
                k, v = kv[line, :, :, 0, head], kv[line, :, :, 0, 2 + head]
            else:
                k, v = kv[:, line, :, 1, head], kv[:, line, :, 1, 2 + head]
            k, v = k.reshape(keys_here, HD), v.reshape(keys_here, HD)
            scores = lax.dot_general(
                queries[g], k, (((1,), (1,)), ((), ())), preferred_element_type=f32
            ) * (HD**-0.5 * LOG2E)
            scores = jnp.where(allowed, scores, -1e30)
            top = jnp.max(scores, -1, keepdims=True)
            if step == 0:
                newest = jnp.broadcast_to(top, (group * rows, lanes))
            else:
                newest = jnp.maximum(largest[of(g)].reshape(group * rows, lanes), top)
            wide = jnp.concatenate([newest] * (keys_here // lanes), 1)
            probs = jnp.exp2(scores - wide)
            sums = jnp.sum(probs, -1, keepdims=True)
            mixed_in = jnp.dot(probs.astype(bf16), v, preferred_element_type=f32)
            if step == 0:
                total[of(g)] = stacked(jnp.broadcast_to(sums, (group * rows, lanes)))
                summed[of(g)] = stacked(mixed_in)
            else:
                fade = jnp.exp2(largest[of(g)].reshape(group * rows, lanes) - newest)
                total[of(g)] = stacked(total[of(g)].reshape(group * rows, lanes) * fade + sums)
                summed[of(g)] = stacked(summed[of(g)].reshape(group * rows, lanes) * fade + mixed_in)
            largest[of(g)] = stacked(newest)
            return carry

        lax.fori_loop(0, 2, one_head, 0)

    for half in range(2):
        attend(half, 0)
    kv_gather.pass_on()
    w_gather.send.finish()
    for half in range(2):
        kv_gather.sides(half)
    for half in range(2):
        for step in (3, 1):
            attend(half, step)
    for half in range(2):
        kv_gather.far(half)
    for half in range(2):
        attend(half, 2)

    for g in range(KVH):
        made = (summed[of(g)] / total[of(g)]).reshape(group * rows, lanes)
        for r in range(group):
            span = slice((g * group + r) * HD, (g * group + r + 1) * HD)
            first[:, span] = acts[:, span].astype(f32) + made[r * rows : (r + 1) * rows]

    mixed[...] = rms_norm(first[...], gains[1]).astype(bf16)
    for name in loaded:
        if name not in ("acts", "gains", "w_kv", "up", "down"):
            loads[name].wait()
    transposed = (((1,), (1,)), ((), ()))
    both_vmem[:, 0:32] = lax.dot_general(
        mixed[...], ref["w_bc"][...], transposed, preferred_element_type=f32
    )
    to_scalars = pltpu.make_async_copy(both_vmem, both, ref["load_sem"].at[0])
    to_scalars.start()
    states = 16
    b_rows = lax.dot_general(
        ref["w_bc"][0:states], mixed[...], transposed, preferred_element_type=f32
    )
    low_rank = jnp.dot(mixed[...], ref["dt_in"][...], preferred_element_type=f32).astype(bf16)
    for i in range(blocks):
        span = slice(i * lanes, (i + 1) * lanes)
        raw = jnp.dot(low_rank, ref["dt_out"][:, span], preferred_element_type=f32)
        raw = raw + ref["dt_bias"][:, span]
        step_size = jnp.maximum(raw, 0.0) + jnp.log1p(jnp.exp(-jnp.abs(raw)))
        keep[:, i, :] = jnp.exp(-step_size * ref["decay_rate"][:, span])
        drive[:, i, :] = step_size * mixed[:, span].astype(f32)

    def fade(turn, later):
        t = rows - 1 - turn
        tail[t] = drive[t] * later
        return later * keep[t]

    ref["product"][...] = lax.fori_loop(0, rows, fade, jnp.ones((blocks, lanes), f32))

    def two_parts(value):
        high = value.astype(bf16)
        return high, (value - high.astype(f32)).astype(bf16)

    b_high, b_low = two_parts(b_rows)
    b_wide = jnp.concatenate([b_high, b_high, b_low], 1)
    message, inbox, outbox, incoming = ref["message"], ref["inbox"], ref["outbox"], ref["incoming"]
    for i in range(blocks):
        high, low = two_parts(tail[:, i, :])
        ending = jnp.dot(b_wide, jnp.concatenate([high, low, high], 0), preferred_element_type=f32)
        for part in range(2):
            message[2 * i + part, 0] = ending[part * 8 : part * 8 + 8]
            message[2 * i + part, 1] = jnp.broadcast_to(ref["product"][i : i + 1], (8, lanes))

    def swap(mine, theirs, semaphore):
        own = pltpu.make_async_copy(mine(ctx), theirs(ctx), ref["scan_recv"].at[semaphore])
        own.start()

        def one(step, carry):
            peer = lax.rem(ctx + step, devices)
            pltpu.make_async_remote_copy(
                src_ref=mine(peer),
                dst_ref=theirs(ctx),
                send_sem=ref["scan_send"].at[semaphore],
                recv_sem=ref["scan_recv"].at[semaphore],
                device_id={"ctx": peer},
                device_id_type=pl.DeviceIdType.MESH,
            ).start()
            return carry

        lax.fori_loop(1, devices, one, 0)

    def advance(t, carry):
        state, product = carry
        kept, driven = keep[t], drive[t]
        state = tuple(s * kept + driven * both[t, n] for n, s in enumerate(state))
        terms = [s * both[t, states + n] for n, s in enumerate(state)]
        while len(terms) > 1:
            terms = [a + b for a, b in zip(terms[::2], terms[1::2])]
        product = product * kept
        drive[t] = terms[0]
        keep[t] = product
        return state, product

    def join(turn, entering):
        outbox[turn] = entering
        return inbox[turn, 1] * entering + inbox[turn, 0]

    def slot(j):
        return incoming.at[
            pl.ds(pl.multiple_of(lax.rem(j, 2) * 8, 8), 8),
            pl.ds(pl.multiple_of(lax.div(j, 2) * lanes, lanes), lanes),
        ]

    swap(lambda j: message.at[j], lambda j: inbox.at[j], 0)
    to_scalars.wait()
    zero = jnp.zeros((blocks, lanes), f32)
    held = ((zero,) * states, jnp.ones((blocks, lanes), f32))
    held = lax.fori_loop(0, rows // 2, advance, held)
    arrived(inbox, ref["scan_recv"].at[0])
    lax.fori_loop(0, devices, join, jnp.zeros((8, lanes), f32))
    swap(lambda j: outbox.at[j], slot, 1)
    lax.fori_loop(rows // 2, rows, advance, held)
    arrived(incoming, ref["scan_recv"].at[1])
    c_high, c_low = two_parts(both_vmem[:, states : 2 * states])
    c_wide = jnp.concatenate([c_high, c_high, c_low], 1)
    for i in range(blocks):
        span = slice(i * lanes, (i + 1) * lanes)
        high, low = two_parts(incoming[:, span])
        carried = jnp.dot(c_wide, jnp.concatenate([high, low, high], 0), preferred_element_type=f32)
        second[:, span] = (
            first[:, span]
            + drive[:, i, :]
            + keep[:, i, :] * carried
            + ref["skip_gain"][:, span] * mixed[:, span].astype(f32)
        )

    normed[...] = rms_norm(second[...], gains[2]).astype(bf16)
    logits = lax.dot_general(
        ref["w_router"][...], normed[...], transposed, preferred_element_type=f32
    )
    expert = lax.broadcasted_iota(jnp.int32, (EXPERTS, rows), 0)
    hits = [(ref["routes"][i : i + 1] == expert).astype(f32) for i in range(2)]
    chosen = [jnp.sum(hit * logits, 0, keepdims=True) for hit in hits]
    top = jnp.maximum(chosen[0], chosen[1])
    powers = [jnp.exp(c - top) for c in chosen]
    share = powers[0] + powers[1]
    gates = hits[0] * (powers[0] / share) + hits[1] * (powers[1] / share)
    hit = hits[0] + hits[1]
    row_at = lax.broadcasted_iota(jnp.int32, (rows, rows), 0)
    col_at = lax.broadcasted_iota(jnp.int32, (rows, rows), 1)
    earlier = (row_at < col_at).astype(bf16)
    rank = jnp.dot(hit.astype(bf16), earlier, preferred_element_type=f32)
    capacity = rows * 2 // EXPERTS
    slots = lax.broadcasted_iota(jnp.int32, (capacity, rows), 0).astype(f32)
    placing = []
    for e in range(EXPERTS):
        taken = (slots == rank[e : e + 1]).astype(f32) * hit[e : e + 1]
        weighting[e * capacity : (e + 1) * capacity] = taken * gates[e : e + 1]
        placing.append(taken.astype(bf16))
    placing = jnp.concatenate(placing, 0)
    for j in range(4):
        span = slice(j * width // 4, (j + 1) * width // 4)
        packed[:, :, :, :, span] = (
            jnp.dot(placing, normed[:, span], preferred_element_type=f32)
            .astype(bf16)
            .reshape(EXPERTS, 2, 2, 16, width // 4)
        )


def experts(ref):
    y, x, core = coordinates()
    left = lax.rem(x + X_CHIPS - 1, X_CHIPS)
    right = lax.rem(x + 1, X_CHIPS)
    far = lax.rem(x + 2, X_CHIPS)
    chips = (x, left, right, far)
    on_left, on_right, on_core = place(y, left, core), place(y, right, core), place(y, x, 1 - core)
    segments = lax.axis_size("segment")
    ahead = {"segment": lax.rem(lax.axis_index("segment") + 1, segments)}
    send, rows, parts, sibling_parts = ref["send"], ref["rows"], ref["parts"], ref["weights"]
    far_parts, side_parts, hidden, packed = ref["far_parts"], ref["side_parts"], ref["hidden"], ref["packed"]
    out = ref["out"]
    f32, bf16 = jnp.float32, jnp.bfloat16
    capacity, width = far_parts.shape[1:]
    strip = width // 2
    strips = [pl.ds(j * strip, strip) for j in range(2)]

    def row_of(k):
        return lax.rem(y + k, Y_CHIPS)

    def block(at, k):
        return rows.at[chips[at], core, row_of(k)]

    def own_block(k):
        send(block(0, k), block(0, k), ref["send_side"].at[0, k], ref["recv_side"].at[0, k], on_right)
        send(block(0, k), block(0, k), ref["send_side"].at[1, k], ref["recv_side"].at[1, k], on_left)
        send(block(0, k), block(0, k), ref["send_core"].at[0, k], ref["recv_core"].at[0, k], on_core)

    def side_block(k):
        arrived(block(1, k), ref["recv_side"].at[0, k])
        if k in (0, 1):
            send(block(1, k), block(1, k), ref["send_far"].at[k], ref["recv_far"].at[k], on_right)
        send(block(1, k), block(1, k), ref["send_core"].at[1, k], ref["recv_core"].at[1, k], on_core)
        arrived(block(2, k), ref["recv_side"].at[1, k])
        if k in (2, 3):
            send(block(2, k), block(2, k), ref["send_far"].at[k], ref["recv_far"].at[k], on_left)
        send(block(2, k), block(2, k), ref["send_core"].at[2, k], ref["recv_core"].at[2, k], on_core)

    def far_block(k):
        arrived(block(3, k), ref["recv_far"].at[k])
        send(block(3, k), block(3, k), ref["send_core"].at[3, k], ref["recv_core"].at[3, k], on_core)

    def from_core(at):
        for k in range(Y_CHIPS):
            other = rows.at[chips[at], 1 - core, row_of(k)]
            arrived(other, ref["recv_core"].at[at, k])

    def multiply(at):
        chip = chips[at]
        taken = [rows[chip, which].reshape(-1, width) for which in (1 - core, core)]
        lifted = jnp.dot(jnp.concatenate(taken, 0), ref["up"][...], preferred_element_type=f32)
        hidden[...] = jax.nn.silu(lifted).astype(bf16)
        half = hidden.shape[0] // 2
        for j, span in enumerate(strips):
            lowered = jnp.dot(hidden[...], ref["down"][:, span], preferred_element_type=f32)
            lowered = lowered.astype(bf16).reshape(2, Y_CHIPS, capacity, strip)
            rows[chip, 1 - core, :, :, :, :, span] = lowered[0].reshape(Y_CHIPS, 2, 2, 16, strip)
            parts[chip, :, :, span] = lowered[1]
            send(
                rows.at[chip, 1 - core, :, :, :, :, span],
                sibling_parts.at[chip, :, :, :, :, span],
                ref["back_core_send"].at[at, j],
                ref["back_core_recv"].at[at, j],
                on_core,
            )

    def mine(at, k, j):
        return parts.at[chips[at], row_of(k), :, strips[j]]

    def total(at, k, j, *more):
        theirs = sibling_parts[chips[at], row_of(k), :, :, :, strips[j]].reshape(capacity, strip)
        made = mine(at, k, j)[...].astype(f32) + theirs.astype(f32)
        for slot in more:
            made = made + slot[...].astype(f32)
        return made.astype(bf16)

    for k in (1, 3, 2):
        send(
            packed.at[row_of(k)],
            rows.at[x, core, y],
            ref["send_y"].at[k],
            ref["recv_y"].at[4 - k],
            place(row_of(k), x, core),
        )
    rows[x, core, y] = packed[y]
    own_block(0)
    for k in (1, 3, 2):
        arrived(block(0, k), ref["recv_y"].at[k])
        own_block(k)
    side_block(0)
    ref["loads"]["up"].wait()
    ref["loads"]["down"].wait()
    from_core(0)
    multiply(0)
    for k in (1, 3, 2):
        side_block(k)
    from_core(1)
    multiply(1)
    far_block(0)
    from_core(2)
    multiply(2)

    def core_sum(at, j):
        arrived(sibling_parts.at[chips[at], :, :, :, :, strips[j]], ref["back_core_recv"].at[at, j])

    def to_side(at, k, j, relayed):
        more = ()
        if relayed:
            slot = far_parts.at[k, :, strips[j]]
            arrived(slot, ref["back_far_recv"].at[k, j])
            more = (slot,)
        mine(at, k, j)[...] = total(at, k, j, *more)
        send(
            mine(at, k, j),
            side_parts.at[at - 1, k, :, strips[j]],
            ref["back_side_send"].at[at - 1, k, j],
            ref["back_side_recv"].at[at - 1, k, j],
            on_left if at == 1 else on_right,
        )

    for k in (1, 3, 2):
        far_block(k)
    for j in range(2):
        core_sum(1, j)
        core_sum(2, j)
        for k in (3, 0):
            to_side(1, k, j, False)
        for k in (2, 1):
            to_side(2, k, j, False)
    from_core(3)
    multiply(3)
    for j in range(2):
        core_sum(3, j)
        for k in (2, 3, 1, 0):
            mine(3, k, j)[...] = total(3, k, j)
            send(
                mine(3, k, j),
                far_parts.at[k, :, strips[j]],
                ref["back_far_send"].at[k, j],
                ref["back_far_recv"].at[k, j],
                on_left if k in (2, 1) else on_right,
            )
    for j in range(2):
        core_sum(0, j)
        for k in (2, 3, 1, 0):
            to_side(1 if k in (2, 1) else 2, k, j, True)
    gate = ref["weighting"][...]
    high = gate.astype(bf16)
    low = (gate - high.astype(f32)).astype(bf16)
    over_slots = (((0,), (0,)), ((), ()))
    for j, span in enumerate(strips):
        for k in (2, 3, 1, 0):
            sides = [side_parts.at[at, k, :, span] for at in range(2)]
            for at in range(2):
                arrived(sides[at], ref["back_side_recv"].at[at, k, j])
            made = total(0, k, j, *sides)
            if k == 0:
                out[y, :, span] = made
            else:
                mine(0, k, j)[...] = made
                send(
                    mine(0, k, j),
                    out.at[y, :, span],
                    ref["back_y_send"].at[k, j],
                    ref["back_y_recv"].at[4 - k, j],
                    place(row_of(k), x, core),
                )
        for k in (1, 3, 2):
            arrived(out.at[row_of(k), :, span], ref["back_y_recv"].at[k, j])
        expert_out = out[:, :, span].reshape(-1, strip)
        summed = lax.dot_general(high, expert_out, over_slots, preferred_element_type=f32)
        summed = summed + lax.dot_general(low, expert_out, over_slots, preferred_element_type=f32)
        ref["finished"][:, span] = (ref["second"][:, span] + summed).astype(bf16)
        send(
            ref["finished"].at[:, span],
            ref["handed"].at[:, span],
            ref["hand_send"].at[j],
            ref["hand_recv"].at[j],
            ahead,
        )
    for j, span in enumerate(strips):
        arrived(ref["handed"].at[:, span], ref["hand_recv"].at[j])
    send.finish()
    count = 2 * X_CHIPS * Y_CHIPS - 1
    arrived(ref["inbox"].at[pl.ds(0, count)], ref["scan_send"].at[0])
    arrived(ref["outbox"].at[pl.ds(0, count)], ref["scan_send"].at[1])


GATHER_SEMS = {"s1": (2, 3), "r1": (2, 3), "s2": (2, 4, 3), "r2": (2, 4, 3), "sc": (2, 4), "rc": (2, 4)}


def layer(**given):
    rows, width = given["acts"].shape
    units = given["up"].shape[1]
    f32, bf16 = jnp.float32, jnp.bfloat16
    vmem = pltpu.VMEM
    capacity = rows * 2 // EXPERTS
    devices = 2 * X_CHIPS * Y_CHIPS
    blocks = width // 128
    grid = (Y_CHIPS, X_CHIPS, 2, 2)
    block = (capacity, width)
    scratch = {name: vmem(value.shape, value.dtype) for name, value in given.items()}
    scratch |= {
        "weights": vmem(grid + (16, width), bf16),
        "kv": vmem(grid + (4, rows, HD), bf16),
        "normed": vmem((rows, width), bf16),
        "queries": vmem((KVH, HEADS // KVH * rows, HD), bf16),
        "first": vmem((rows, width), f32),
        "mixed": vmem((rows, width), bf16),
        "keep": vmem((rows, blocks, 128), f32),
        "drive": vmem((rows, blocks, 128), f32),
        "tail": vmem((rows, blocks, 128), f32),
        "product": vmem((blocks, 128), f32),
        "both_vmem": vmem((rows, 128), f32),
        "both": pltpu.SMEM((rows, 128), f32),
        "message": vmem((devices, 2, 8, 128), f32),
        "inbox": vmem((devices, 2, 8, 128), f32),
        "outbox": vmem((devices, 8, 128), f32),
        "incoming": vmem((16, width), f32),
        "second": vmem((rows, width), f32),
        "packed": vmem((EXPERTS, 2, 2, 16, width), bf16),
        "weighting": vmem((EXPERTS * capacity, rows), f32),
        "rows": vmem((X_CHIPS, 2, Y_CHIPS, 2, 2, 16, width), bf16),
        "parts": vmem((X_CHIPS, Y_CHIPS) + block, bf16),
        "far_parts": vmem((Y_CHIPS,) + block, bf16),
        "side_parts": vmem((2, Y_CHIPS) + block, bf16),
        "hidden": vmem((2 * Y_CHIPS * capacity, units), bf16),
        "out": vmem((EXPERTS,) + block, bf16),
        "finished": vmem((rows, width), bf16),
    }
    sems = {
        "load_sem": (len(given),),
        "scan_send": (2,),
        "scan_recv": (2,),
        "send_y": (4,),
        "recv_y": (4,),
        "send_side": (2, 4),
        "recv_side": (2, 4),
        "send_far": (4,),
        "recv_far": (4,),
        "send_core": (4, 4),
        "recv_core": (4, 4),
        "back_core_send": (4, 2),
        "back_core_recv": (4, 2),
        "back_far_send": (4, 2),
        "back_far_recv": (4, 2),
        "back_side_send": (2, 4, 2),
        "back_side_recv": (2, 4, 2),
        "back_y_send": (4, 2),
        "back_y_recv": (4, 2),
        "hand_send": (2,),
        "hand_recv": (2,),
    }
    for gather in ("w_", "kv_"):
        sems |= {gather + name: shape for name, shape in GATHER_SEMS.items()}
    scratch |= {name: pltpu.SemaphoreType.DMA(shape) for name, shape in sems.items()}
    names = [name + "_any" for name in given] + ["handed"] + list(scratch)
    return pl.pallas_call(
        functools.partial(layer_kernel, names),
        out_shape=jax.ShapeDtypeStruct((rows, width), bf16),
        in_specs=[pl.BlockSpec(memory_space=pl.ANY)] * len(given),
        out_specs=pl.BlockSpec(memory_space=pltpu.VMEM),
        scratch_shapes=list(scratch.values()),
        compiler_params=pltpu.CompilerParams(
            collective_id=1, has_side_effects=True, vmem_limit_bytes=60 * MIB
        ),
        name="layer",
    )(*given.values())


def on_device(
    acts,
    norm_gains,
    w_kv,
    dt_in,
    dt_out,
    dt_bias,
    decay_rate,
    w_bc,
    skip_gain,
    w_router,
    routes,
    w_up,
    w_down,
):
    return layer(
        acts=acts[0],
        gains=norm_gains.transpose(1, 0, 2),
        w_kv=w_kv[0].T,
        dt_bias=dt_bias,
        decay_rate=decay_rate,
        skip_gain=skip_gain,
        routes=routes[0].T,
        dt_in=dt_in[0],
        dt_out=dt_out[0],
        w_bc=w_bc[0].T,
        w_router=w_router[0].T,
        up=w_up[0],
        down=w_down[0],
    )[None]


def solution(mesh):
    in_specs = (
        P("segment", "ctx", None),
        P("segment", None, None),
        P("segment", None, "ctx"),
        P("segment", None, None),
        P("segment", None, None),
        P("segment", None),
        P("segment", None),
        P("segment", None, None),
        P("segment", None),
        P("segment", None, None),
        P("segment", "ctx", None),
        P("segment", None, "ctx"),
        P("segment", "ctx", None),
    )
    out_specs = P("segment", "ctx", None)
    return jax.shard_map(
        on_device, mesh=mesh, in_specs=in_specs, out_specs=out_specs, check_vma=False
    )
```

time: 553 us -> 179 us (0.32); the launches traced: 547 us -> 179 us
  waiting for transfers between devices: 259 us -> 0 us
  Pallas kernels: 0 us -> 177 us
  blocking collectives: 127 us -> 0 us
  matrix products: 83 us -> 0 us
  other arithmetic: 40.9 us -> 0 us
  local copies, waits for them, and re-layouts: 15.8 us -> 1.88 us
  between operations: 13.5 us -> 0.01 us
  starting transfers between devices: 6.83 us -> 0 us
    pallas_call x0 -> x1, Pallas kernels: none -> 177 us  [layer(): pl.pallas_call(functools.partial(layer_kernel, names), out_shape=jax.Shap...]
    all_gather x4 -> x0, waiting for transfers between devices: 151 us -> none  [the longest x1 56 us: on_device(): lax.all_gather(w_kv[0], 'ctx', axis=1, tiled=True)]
    all_to_all x1 -> x0, blocking collectives: 103 us -> none  [on_device(): lax.all_to_all(outgoing, 'ctx', split_axis=0, concat_axis=0, tiled=True)]
    all_to_all x1 -> x0, waiting for transfers between devices: 99.1 us -> none  [on_device(): lax.all_to_all(part_out, 'ctx', split_axis=0, concat_axis=0, tiled=True)]
    dot_general x26 -> x0, matrix products: 83 us -> none  [the longest x1 24.2 us: on_device(): jnp.dot(hidden, down_local, preferred_element_type=jnp.float32)]
    reduce_sum x10 -> x0, other arithmetic: 32.1 us -> none  [the longest x1 14.7 us: on_device(): total = jnp.sum(weights, -1)]
    all_gather x1 -> x0, blocking collectives: 24 us -> none  [entering(): lax.all_gather(a.astype(kind), axis)]
    ppermute x1 -> x0, waiting for transfers between devices: 8.33 us -> none  [shifted(): return lax.ppermute(value, axis, pairs)]
  transfers between devices with their start and end apart: 6 -> 0, of which waited for: 6 -> 0; matrix products, arithmetic and copies ran while one was open for 7% -> 0% of each run, Pallas kernels for 0% -> 0%
where the time goes in v3:
time: 179 us
  Pallas kernels  177 us (99%)
  local copies, waits for them, and re-layouts  1.88 us (1%)
    pallas_call x1, Pallas kernels, layer(): pl.pallas_call(functools.partial(layer_kernel, names), out_shape=jax.Shap...  177 us

profile of v3, /device:TPU:1, one launch (start us, length us, event | category | flops | bytes accessed | tf_op | source)
XLA Modules:
  0.0 178.8 jit_solution(12456829793028230532)
XLA Ops:
  0.0 176.9 %layer.1 = bf16[128,2048]{1,0:T(8,128)(2,1)} custom-call(bf16[128,2048]{1,0:T(8,128)(2,1)} %bitcast.22, f32[3,1,2048]{2,1,0:T(1,128)} %bitcast.27, bf16[32,2048]{1,0:T(8,128)(2,1)} %bitcast.25, f32[1,2048]{1,0:T(1,128)} %refs_3_.1, f32[1,2048]{1,0:T(1,128)} %refs_4_.1, f32[1,2048]{1,0:T(1,128)} %refs_5_.1, s32[2,128]{1,0:T(2,128)} %bitcast.29, ...), custom_call_target="tpu_custom_call" | custom-call | tf_op jit(solution)/shard_map/layer/pallas_call | solution.py:707
  176.9 1.9 %copy.15 = bf16[1,128,2048]{2,1,0:T(8,128)(2,1)} copy(bf16[1,128,2048]{2,1,0:T(8,128)(2,1)} %bitcast.21) | data formatting | bytes 1048576
